TPU v7x, 128 devices: a whole 4x4x4 slice. The times are simulated.
128 devices in a mesh: adapter: 16 (over y, z), tensor: 8 (over x, core).
Axes of the slice: x: 4, y: 4, z: 4, core: 2. Of those that a mesh axis runs over, the one named last changes fastest.
Arguments:
- tokens: bfloat16 [1024, 8192], P('adapter', 'tensor'), may hold values from -6 to 6
- token_adapter: int32 [1024], P('adapter'), may hold values from 0 to 31, as said below
- adapter_slot_table: int32 [32], replicated, may hold values from 0 to 31, each once
- gate_matrix: bfloat16 [8192, 28672], P(None, ('adapter', 'tensor')), may hold values from -0.0625 to 0.0625
- up_matrix: bfloat16 [8192, 28672], P(None, ('adapter', 'tensor')), may hold values from -0.0625 to 0.0625
- down_matrix: bfloat16 [28672, 8192], P(('adapter', 'tensor')), may hold values from -0.03125 to 0.03125
- adapter_entry_maps: bfloat16 [32, 8192, 128], P('adapter'), may hold values from -0.0625 to 0.0625
- adapter_gate_exit: bfloat16 [32, 64, 28672], P(None, None, ('adapter', 'tensor')), may hold values from -0.375 to 0.375
- adapter_up_exit: bfloat16 [32, 64, 28672], P(None, None, ('adapter', 'tensor')), may hold values from -0.375 to 0.375
- adapter_down_entry: bfloat16 [32, 28672, 64], P(None, ('adapter', 'tensor')), may hold values from -0.03125 to 0.03125
- adapter_down_exit: bfloat16 [32, 64, 8192], P('adapter', None, 'tensor'), may hold values from -0.375 to 0.375
Outputs:
- mixed: bfloat16 [1024, 8192], P('adapter', 'tensor')
Inputs may be any that keep to these rules, and one draw needn't show every extreme that they name: `token_adapter`: every adapter is the adapter of 1 to 80 tokens, and some adapter of exactly 80. `adapter_slot_table`: each slot number appears once.
All inputs are finite; a program needn't handle non-finite values.
Results may differ from a plain program's by a relative error of at most 0.0055.
Values may be sent and summed in bfloat16 or wider, within the bound.
No kernel may reach another device: no remote copies, remote signals or barrier semaphores. Data moves between devices by JAX's collectives and lax.ppermute only.
A program may use at most 192 MiB of HBM per device.

v0:
```python
import functools

import jax
import jax.numpy as jnp
from jax import lax
from jax.experimental import pallas as pl
from jax.experimental.pallas import tpu as pltpu
from jax.sharding import PartitionSpec as P

SEGMENT = 80
BF = jnp.bfloat16
F32 = jnp.float32
AXES = ("adapter", "tensor")
VMEM_LIMIT = 60 * 1024 * 1024


def pairs(move):
    out = []
    for i in range(128):
        y, z, x, c = i // 32, (i // 8) % 4, (i // 2) % 4, i % 2
        ty, tz, tx, tc = move(y, z, x, c)
        out.append((i, (ty % 4) * 32 + (tz % 4) * 8 + (tx % 4) * 2 + tc % 2))
    return out


def send(value, dy=0, dz=0, dx=0, dc=0):
    return lax.ppermute(value, AXES, pairs(lambda y, z, x, c: (y + dy, z + dz, x + dx, c + dc)))


def onward(value, axis, step):
    def move(y, z, x, c):
        d = step * (1 - 2 * c)
        return (y + d, z, x, c) if axis == "y" else (y, z + d, x, c)

    return lax.ppermute(value, AXES, pairs(move))


def ring(value, axis):
    return onward(value, axis, 1)


def params(n=1):
    return pltpu.CompilerParams(
        dimension_semantics=("arbitrary",) * n, vmem_limit_bytes=VMEM_LIMIT
    )


def nt(a, b):
    return lax.dot_general(a, b, (((1,), (1,)), ((), ())), preferred_element_type=F32)


def low_kernel(x_ref, e_ref, s_ref, o_ref, acc):
    k = pl.program_id(0)

    @pl.when(k == 0)
    def _():
        acc[...] = jnp.zeros_like(acc)

    for j in range(2):
        x = x_ref[:, j].reshape(1024, 1024)
        at = pl.ds(1024 * j, 1024)
        e = jnp.concatenate([e_ref[0, at], e_ref[1, at]], axis=1)
        acc[...] += jnp.dot(x, e, preferred_element_type=F32)

    @pl.when(k == pl.num_programs(0) - 1)
    def _():
        for j in range(2):
            o_ref[j] = jnp.dot(
                s_ref[j], acc[:, 128 * j : 128 * (j + 1)].astype(BF), preferred_element_type=F32
            ).astype(BF)


def low_own_rows(every, entry, select):
    return pl.pallas_call(
        low_kernel,
        grid=(4,),
        in_specs=[
            pl.BlockSpec((16, 2, 64, 1024), lambda k: (0, k, 0, 0)),
            pl.BlockSpec((2, 2048, 128), lambda k: (0, k, 0)),
            pl.BlockSpec((2, SEGMENT, 1024), lambda k: (0, 0, 0)),
        ],
        out_specs=pl.BlockSpec((2, SEGMENT, 128), lambda k: (0, 0, 0)),
        out_shape=jax.ShapeDtypeStruct((2, SEGMENT, 128), BF),
        scratch_shapes=[pltpu.VMEM((1024, 256), F32)],
        compiler_params=params(),
        cost_estimate=pl.CostEstimate(
            flops=2 * 1024 * 8192 * 256, bytes_accessed=21 << 20, transcendentals=0
        ),
        name="low_own",
    )(every, entry, select)


def gate_up_kernel(x_ref, g_ref, u_ref, *refs):
    o_ref = refs[-1]
    n = g_ref.shape[0]

    @pl.when(pl.program_id(0) == 0)
    def _():
        o_ref[...] = jnp.zeros_like(o_ref)

    for j in range(2):
        x = x_ref[:, j].reshape(512, 1024)
        at = pl.ds(1024 * j, 1024)
        o_ref[0, :, :n] += nt(x, g_ref[:, at])
        o_ref[0, :, 256 : 256 + n] += nt(x, u_ref[:, at])


def gate_up(every, gate, up, half, sums):
    n = gate.shape[0]
    args = [every, gate, up]
    specs = [
        pl.BlockSpec((8, 2, 64, 1024), lambda k: (half, k, 0, 0)),
        pl.BlockSpec((n, 2048), lambda k: (0, k)),
        pl.BlockSpec((n, 2048), lambda k: (0, k)),
    ]
    if sums is not None:
        args.append(sums)
        specs.append(pl.BlockSpec(memory_space=pl.ANY))
    return pl.pallas_call(
        gate_up_kernel,
        grid=(4,),
        in_specs=specs,
        out_specs=pl.BlockSpec((1, 512, 512), lambda k: (half, 0, 0)),
        out_shape=jax.ShapeDtypeStruct((2, 512, 512), F32),
        input_output_aliases={} if sums is None else {3: 0},
        compiler_params=params(),
        cost_estimate=pl.CostEstimate(
            flops=1024 * 8192 * 512, bytes_accessed=16 << 20, transcendentals=0
        ),
        name="gate_up",
    )(*args)


def hidden_kernel(
    place, a_ref, slot_ref, row_ref, low_ref, ge_ref, ue_ref, de_ref, h_ref, t_ref
):
    lane = lax.broadcasted_iota(jnp.int32, (256, 256), 1)
    row = row_ref[...]
    slot = slot_ref[...]

    def equal(value, index):
        return jnp.where(value == index, 1.0, 0.0)

    low = jnp.zeros((256, 128), F32)
    for j in range(10):
        pick = equal(row, lane + 256 * j).astype(BF)
        low += jnp.dot(pick, low_ref[pl.ds(256 * j, 256)], preferred_element_type=F32)
    lg = low[:, :64].astype(BF)
    lu = low[:, 64:].astype(BF)
    lg = jnp.concatenate([lg] * 4, axis=1)
    lu = jnp.concatenate([lu] * 4, axis=1)
    n = ge_ref.shape[1]
    gate = a_ref[0, :, :n]
    up = a_ref[0, :, 256 : 256 + n]
    for j in range(8):
        mask = equal(slot, lane // 64 + 4 * j).astype(BF)
        gate += jnp.dot(lg * mask, ge_ref[pl.ds(256 * j, 256)], preferred_element_type=F32)
        up += jnp.dot(lu * mask, ue_ref[pl.ds(256 * j, 256)], preferred_element_type=F32)
    hidden = (gate / (1.0 + jnp.exp(-gate)) * up).astype(BF)
    down = jnp.zeros((256, 256), F32)
    for j in range(8):
        mask = equal(slot, lane // 64 + 4 * j)
        down += nt(hidden, de_ref[pl.ds(256 * j, 256)]) * mask
    down = (down[:, :128] + down[:, 128:]).astype(BF)
    wide = jnp.concatenate([hidden, jnp.zeros((256, 256 - hidden.shape[1]), BF), down], axis=1)
    ry = place[pl.program_id(0)]
    for z in range(4):
        rz = place[4 + z]
        upper = wide[64 * z : 64 * z + 32]
        lower = wide[64 * z + 32 : 64 * z + 64]
        h_ref[(rz + 3) % 4, 0, ry] = upper
        h_ref[(ry + 3) % 4, 1, rz] = lower
        t_ref[(7 - rz) % 4, 0, (4 - ry) % 4] = upper
        t_ref[(7 - ry) % 4, 1, (4 - rz) % 4] = lower


def hidden_rows(place, sums, slot, row, low, gate_exit, up_exit, down_entry):
    n = gate_exit.shape[1]
    return pl.pallas_call(
        hidden_kernel,
        grid_spec=pltpu.PrefetchScalarGridSpec(
            num_scalar_prefetch=1,
            grid=(4,),
            in_specs=[
                pl.BlockSpec((1, 256, 512), lambda i, p: (i, 0, 0)),
                pl.BlockSpec((256, 1), lambda i, p: (i, 0)),
                pl.BlockSpec((256, 1), lambda i, p: (i, 0)),
                pl.BlockSpec((2560, 128), lambda i, p: (0, 0)),
                pl.BlockSpec((2048, n), lambda i, p: (0, 0)),
                pl.BlockSpec((2048, n), lambda i, p: (0, 0)),
                pl.BlockSpec((2048, n), lambda i, p: (0, 0)),
            ],
            out_specs=[pl.BlockSpec((4, 2, 4, 32, 384), lambda i, p: (0, 0, 0, 0, 0))] * 2,
        ),
        out_shape=[jax.ShapeDtypeStruct((4, 2, 4, 32, 384), BF)] * 2,
        compiler_params=params(),
        cost_estimate=pl.CostEstimate(
            flops=2 * 1024 * 2560 * 512, bytes_accessed=16 << 20, transcendentals=1024 * n
        ),
        name="hidden_rows",
    )(place, sums, slot, row, low, gate_exit, up_exit, down_entry)


def on_device(
    tokens,
    token_adapter,
    adapter_slot_table,
    gate_matrix,
    up_matrix,
    down_matrix,
    adapter_entry_maps,
    adapter_gate_exit,
    adapter_up_exit,
    adapter_down_entry,
    adapter_down_exit,
):
    units = gate_matrix.shape[1]
    a = lax.axis_index("adapter")
    t = lax.axis_index("tensor")
    y, z, x, c = a // 4, a % 4, t // 2, t % 2
    way = 1 - 2 * c

    every = lax.all_gather(tokens, AXES, axis=0, tiled=False).reshape(16, 8, 64, 1024)
    ids = lax.all_gather(token_adapter, "adapter", axis=0, tiled=True)

    exits = adapter_down_exit
    for axis in "yz":
        exits = [exits]
        for _ in range(3):
            exits.append(ring(exits[-1], axis))
        exits = jnp.stack(exits)
    exits = exits.reshape(2048, 1024)

    names = jnp.arange(32, dtype=jnp.int32)
    member = ids[:, None] == names[None, :]
    order = jnp.arange(1024, dtype=jnp.int32)
    before = (order[:, None] > order[None, :]).astype(BF)
    earlier = jnp.dot(before, member.astype(BF), preferred_element_type=F32).astype(jnp.int32)
    rank_in = jnp.sum(jnp.where(member, earlier, 0), axis=1)
    slot = jnp.sum(jnp.where(member, adapter_slot_table[None, :], 0), axis=1)
    owner = slot // 2
    row = (slot % 2) * SEGMENT + rank_in
    select = (
        (jnp.where(owner == a, row, -1))[None, :] == jnp.arange(160, dtype=jnp.int32)[:, None]
    ).astype(BF).reshape(2, SEGMENT, 1024)
    relative = ((owner % 4 - z) % 4) * 4 + (owner // 4 - y) % 4

    def column(r, core):
        at = ((x + r) % 4 * 2 + core) * 1024
        return lax.dynamic_slice(down_matrix, (0, at), (units, 1024))

    turns = (1, 2, 3, 0)
    def columns(turns, core, rows, extra):
        width = 1024 * len(turns)
        if extra:
            out = jnp.pad(jnp.eye(128, dtype=BF), ((rows - 128, 0), (width, 0)))
        else:
            out = jnp.zeros((rows, width), BF)
        for i, r in enumerate(turns):
            out = lax.dynamic_update_slice(out, column(r, core), (0, 1024 * i))
        return out

    theirs = columns(turns, 1 - c, 384, True)
    mine = (columns((1, 2), c, 256, False), columns((3, 0), c, 384, True))

    every, exits, select, slot, row, theirs, mine = lax.optimization_barrier(
        (every, exits, select, slot, (relative * 160 + row)[:, None], theirs, mine)
    )
    low_own = low_own_rows(every, adapter_entry_maps, select).reshape(160, 128)
    low = jnp.stack([low_own] + [send(low_own, dy=-d) for d in (1, 2, 3)])
    low = jnp.stack([low] + [send(low, dz=-d) for d in (1, 2, 3)]).reshape(2560, 128)
    sums = None
    for half in range(2):
        sums = gate_up(every, gate_matrix.T, up_matrix.T, half, sums)
    sums = sums.reshape(4, 256, 512)

    quarter = jnp.arange(4, dtype=jnp.int32)
    place = jnp.concatenate([way * (y - quarter) % 4, way * (z - quarter) % 4])
    rows, back = hidden_rows(
        place,
        sums,
        slot[:, None],
        row,
        low,
        adapter_gate_exit.reshape(2048, units),
        adapter_up_exit.reshape(2048, units),
        adapter_down_entry.transpose(0, 2, 1).reshape(2048, units),
    )
    rows = rows.reshape(4, 2, 128, 384)
    back = back.reshape(4, 256, 384)
    first = jnp.dot(back[0], theirs, preferred_element_type=F32).astype(BF)
    back, first = lax.optimization_barrier((back, first))
    rest = jnp.dot(back[1:].reshape(768, 384), theirs, preferred_element_type=F32).astype(BF)
    rest, first_other = lax.optimization_barrier((rest, send(first, dc=1)))
    others = jnp.split(send(rest, dc=1).reshape(3, 2, 128, 4224), 3)
    others = [first_other.reshape(1, 2, 128, 4224)] + others

    axes = (("z", "y"), ("y", "z"))
    spans = ((0, 2048), (2048, 4224))

    def own_part(rows, step, ch, color, lo=0, hi=128):
        h = rows[step, color, lo:hi, : mine[ch].shape[0]]
        part = jnp.dot(h, mine[ch], preferred_element_type=F32)
        return part + others[step][0, color, lo:hi, slice(*spans[ch])].astype(F32)

    chains = [(ch, color) for ch in range(2) for color in range(2)]
    came = {k: own_part(rows, 0, *k).astype(BF) for k in chains}
    rows, came = lax.optimization_barrier((rows, came))
    came = {k: ring(v, axes[k[1]][0]) for k, v in came.items()}
    for step in range(1, 3):
        for ch, color in chains:
            total = own_part(rows, step, ch, color) + came[ch, color].astype(F32)
            came[ch, color] = ring(total.astype(BF), axes[color][0])
    summed = []
    for color in range(2):
        parts = {}
        for r in turns:
            lo, hi = 32 * r, 32 * r + 32
            parts[r] = jnp.concatenate(
                [
                    own_part(rows, 3, ch, color, lo, hi) + came[ch, color][lo:hi].astype(F32)
                    for ch in range(2)
                ],
                axis=1,
            )
        total = parts[0]
        for r in (1, 2, 3):
            total += onward(parts[r].astype(BF), axes[color][1], -r).astype(F32)
        summed.append(total)
    summed = jnp.concatenate(summed)
    summed = (summed[:, :2048], summed[:, 2048:])
    tail = summed[1][:, 2048:]
    blocks = {
        1: summed[0][:, :1024],
        2: summed[0][:, 1024:],
        3: summed[1][:, :1024],
        0: summed[1][:, 1024:2048],
    }
    total = jnp.concatenate([blocks[0], tail], axis=1)
    for r in (1, 2, 3):
        total = total + send(
            jnp.concatenate([blocks[r], tail], axis=1).astype(BF), dx=r
        ).astype(F32)

    own_slot = jnp.sum(
        jnp.where(token_adapter[:, None] == names[None, :], adapter_slot_table[None, :], 0), axis=1
    )
    low_down = total[:, 1024:].astype(BF)
    ry = way * (y - own_slot // 8) % 4
    rz = way * (z - own_slot // 2 % 4) % 4
    at = jnp.arange(2048, dtype=jnp.int32) // 128
    spread = jnp.where((rz * 4 + ry)[:, None] == at[None, :], jnp.tile(low_down, (1, 16)), 0)
    delta = jnp.dot(spread, exits, preferred_element_type=F32)
    return (total[:, :1024] + delta).astype(BF)


def solution(mesh):
    return jax.shard_map(
        on_device,
        mesh=mesh,
        in_specs=(
            P("adapter", "tensor"),
            P("adapter"),
            P(),
            P(None, ("adapter", "tensor")),
            P(None, ("adapter", "tensor")),
            P(("adapter", "tensor"), None),
            P("adapter", None, None),
            P(None, None, ("adapter", "tensor")),
            P(None, None, ("adapter", "tensor")),
            P(None, ("adapter", "tensor"), None),
            P("adapter", None, "tensor"),
        ),
        out_specs=P("adapter", "tensor"),
        check_vma=False,
    )
```

profile of v0, /device:TPU:0, one launch (start us, length us, event | category | flops | bytes accessed | tf_op | source)
XLA Modules:
  0.0 249.2 jit_solution(10362774709796605677)
XLA Ops:
  9.0 6.1 %collective-permute-done = bf16[2,64,1024]{2,1,0:T(8,128)(2,1)S(1)} collective-permute-done((bf16[2,64,1024]{2,1,0:T(8,128)(2,1)}, bf16[2,64,1024]{2,1,0:T(8,128)(2,1)S(1)}, u32[]{:S(2)}, u32[]{:S(2)}) %collective-permute-start) | collective-permute-done | bytes 262176 | tf_op jit(solution)/shard_map/ppermute | solution.py:35
  15.6 7.1 %collective-permute-done.1 = bf16[2,64,1024]{2,1,0:T(8,128)(2,1)S(1)} collective-permute-done((bf16[2,64,1024]{2,1,0:T(8,128)(2,1)S(1)}, bf16[2,64,1024]{2,1,0:T(8,128)(2,1)S(1)}, u32[]{:S(2)}, u32[]{:S(2)}) %collective-permute-start.1) | collective-permute-done | bytes 262176 | tf_op jit(solution)/shard_map/ppermute | solution.py:35
  22.7 8.0 %collective-permute-done.2 = bf16[2,64,1024]{2,1,0:T(8,128)(2,1)S(1)} collective-permute-done((bf16[2,64,1024]{2,1,0:T(8,128)(2,1)S(1)}, bf16[2,64,1024]{2,1,0:T(8,128)(2,1)S(1)}, u32[]{:S(2)}, u32[]{:S(2)}) %collective-permute-start.2) | collective-permute-done | bytes 262176 | tf_op jit(solution)/shard_map/ppermute | solution.py:35
  30.7 2.1 fusion.217
  34.6 16.8 %collective-permute-done.3 = bf16[4,2,64,1024]{3,2,1,0:T(8,128)(2,1)S(1)} collective-permute-done((bf16[4,2,64,1024]{3,2,1,0:T(8,128)(2,1)S(1)}, bf16[4,2,64,1024]{3,2,1,0:T(8,128)(2,1)S(1)}, u32[]{:S(2)}, u32[]{:S(2)}) %collective-permute-start.3) | collective-permute-done | bytes 1048608 | tf_op jit(solution)/shard_map/ppermute | solution.py:35
  55.2 18.7 %all-reduce.3 = s32[1024]{0:T(1024)S(1)} all-reduce(s32[1024]{0:T(1024)S(1)} %dynamic-update-slice), channel_id=1, replica_groups=mesh['adapter'=16,'tensor'=8] {'adapter'}, use_global_device_ids=true, to_apply=%add.3 | all-reduce | flops 1024 | bytes 8192
  76.0 2.1 dynamic-slice_dynamic-update-slice_fusion.5
  78.6 2.3 dynamic-slice_dynamic-update-slice_fusion.1
  80.9 3.0 %collective-permute-start.5 = (bf16[4,2,64,1024]{3,2,1,0:T(8,128)(2,1)}, bf16[4,2,64,1024]{3,2,1,0:T(8,128)(2,1)}, u32[]{:S(2)}, u32[]{:S(2)}) collective-permute-start(bf16[4,2,64,1024]{3,2,1,0:T(8,128)(2,1)} %collective-permute-done.4), channel_id=1, source_target_pairs={{0,8},{1,25},{2,10},{3,27},{4,12},{5,29},{6,14},{7,31},{8,16},{9,1... | collective-permute-start | bytes 3145736 | tf_op jit(solution)/shard_map/ppermute | solution.py:35
  86.0 2.4 dynamic-slice_dynamic-update-slice_fusion
  89.2 2.2 fusion.34.row_ref
  91.4 12.0 %collective-permute-done.5 = bf16[4,2,64,1024]{3,2,1,0:T(8,128)(2,1)} collective-permute-done((bf16[4,2,64,1024]{3,2,1,0:T(8,128)(2,1)}, bf16[4,2,64,1024]{3,2,1,0:T(8,128)(2,1)}, u32[]{:S(2)}, u32[]{:S(2)}) %collective-permute-start.5) | collective-permute-done | bytes 1048608 | tf_op jit(solution)/shard_map/ppermute | solution.py:35
  103.4 3.5 %pad_maximum_fusion = bf16[4,4,2,64,1024]{4,3,2,1,0:T(8,128)(2,1)} fusion(bf16[1,4,2,64,1024]{4,3,2,1,0:T(8,128)(2,1)} %bitcast.8, bf16[1,4,2,64,1024]{4,3,2,1,0:T(8,128)(2,1)} %bitcast.7, bf16[1,4,2,64,1024]{4,3,2,1,0:T(8,128)(2,1)S(1)} %bitcast.411, bf16[1,4,2,64,1024]{4,3,2,1,0:T(8,128)(2,1)S(1)} %copy-done.2), kind=kLoop, calls=%fused_computation.2 | loop fusion | flops 6291456 | bytes 8388608 | tf_op jit(solution)/shard_map/stack | solution.py:231
  106.9 10.2 %low_own.1 = bf16[2,80,128]{2,1,0:T(8,128)(2,1)} custom-call(bf16[16,8,64,1024]{3,2,1,0:T(8,128)(2,1)} %bitcast.347, bf16[2,8192,128]{2,1,0:T(8,128)(2,1)} %e_ref.1, bf16[2,80,1024]{2,1,0:T(8,128)(2,1)} %compare_convert_fusion.s_ref), custom_call_target="tpu_custom_call" | custom-call | flops 4294967296 | bytes 22020096 | tf_op jit(solution)/shard_map/low_own/pallas_call | solution.py:74
  117.1 2.7 %collective-permute-start.6 = (bf16[160,128]{1,0:T(8,128)(2,1)}, bf16[160,128]{1,0:T(8,128)(2,1)S(1)}, u32[]{:S(2)}, u32[]{:S(2)}) collective-permute-start(bf16[160,128]{1,0:T(8,128)(2,1)} %bitcast.420), channel_id=1, source_target_pairs={{0,96},{1,97},{2,98},{3,99},{4,100},{5,101},{6,102},{7,103},{8,104... | collective-permute-start | bytes 122888 | tf_op jit(solution)/shard_map/ppermute | solution.py:27
  121.5 9.3 %gate_up.2.refs_0_ = f32[2,512,512]{2,1,0:T(8,128)} custom-call(bf16[16,8,64,1024]{3,2,1,0:T(8,128)(2,1)} %bitcast.348, bf16[224,8192]{1,0:T(8,128)(2,1)} %bitcast.351, bf16[224,8192]{1,0:T(8,128)(2,1)} %bitcast.353), custom_call_target="tpu_custom_call" | custom-call | flops 4294967296 | bytes 16777216 | tf_op jit(solution)/shard_map/gate_up/pallas_call | solution.py:119
  133.0 9.2 %gate_up.3 = f32[2,512,512]{2,1,0:T(8,128)} custom-call(bf16[16,8,64,1024]{3,2,1,0:T(8,128)(2,1)} %bitcast.349, bf16[224,8192]{1,0:T(8,128)(2,1)} %bitcast.352, bf16[224,8192]{1,0:T(8,128)(2,1)} %bitcast.354, f32[2,512,512]{2,1,0:T(8,128)} %gate_up.2.refs_0_), custom_call_target="tpu_custom_call", output_to_operand_aliasing={{}: (3, {})} | custom-call | flops 4294967296 | bytes 16777216 | tf_op jit(solution)/shard_map/gate_up/pallas_call | solution.py:119
  144.2 10.9 %hidden_rows.1 = (bf16[4,2,4,32,384]{4,3,2,1,0:T(8,128)(2,1)}, bf16[4,2,4,32,384]{4,3,2,1,0:T(8,128)(2,1)}) custom-call(s32[8]{0:T(128)} %pad_add_fusion.place, f32[4,256,512]{2,1,0:T(8,128)} %bitcast.377, s32[1024,1]{1,0:T(8,128)} %copy.24.slot_ref, s32[1024,1]{1,0:T(8,128)} %fusion.34.row_ref, bf16[2560,128]{1,0:T(8,128)(2,1)} %bitcast.414, ...), custom_call_target="tpu_custom_call" | custom-call | flops 2684354560 | bytes 16777216 | tf_op jit(solution)/shard_map/hidden_rows/pallas_call | solution.py:179
  156.1 3.4 %convolution_convert_fusion.1 = bf16[256,4224]{1,0:T(8,128)(2,1)S(1)} fusion(bf16[256,384]{1,0:T(8,128)(2,1)S(1)} %bitcast.412, bf16[384,4224]{1,0:T(8,128)(2,1)} %get-tuple-element.31), kind=kOutput, calls=%fused_computation.1 | convolution fusion | flops 831553536 | bytes 5603328 | tf_op jit(solution)/shard_map/dot_general | solution.py:291
  159.6 5.5 %convolution_convert_fusion = bf16[768,4224]{1,0:T(8,128)(2,1)} fusion(bf16[768,384]{1,0:T(8,128)(2,1)S(1)} %bitcast.415, bf16[384,4224]{1,0:T(8,128)(2,1)S(1)} %copy-done.1), kind=kOutput, calls=%fused_computation | convolution fusion | flops 2494660608 | bytes 10321920 | tf_op jit(solution)/shard_map/dot_general | solution.py:293
  167.3 2.2 collective-permute-start.14
  181.5 2.2 collective-permute-done.17
  189.3 2.2 collective-permute-done.24
  195.3 2.2 collective-permute-done.27
  200.4 2.7 %collective-permute-done.25 = bf16[128,2048]{1,0:T(8,128)(2,1)S(1)} collective-permute-done((bf16[128,2048]{1,0:T(8,128)(2,1)S(1)}, bf16[128,2048]{1,0:T(8,128)(2,1)S(1)}, u32[]{:S(2)}, u32[]{:S(2)}) %collective-permute-start.25) | collective-permute-done | bytes 524320 | tf_op jit(solution)/shard_map/ppermute | solution.py:35
  205.5 3.6 %collective-permute-done.28 = bf16[128,2176]{1,0:T(8,128)(2,1)S(1)} collective-permute-done((bf16[128,2176]{1,0:T(8,128)(2,1)S(1)}, bf16[128,2176]{1,0:T(8,128)(2,1)S(1)}, u32[]{:S(2)}, u32[]{:S(2)}) %collective-permute-start.28) | collective-permute-done | bytes 557088 | tf_op jit(solution)/shard_map/ppermute | solution.py:35
  211.3 2.7 %collective-permute-start.30 = (bf16[32,4224]{1,0:T(8,128)(2,1)S(1)}, bf16[32,4224]{1,0:T(8,128)(2,1)S(1)}, u32[]{:S(2)}, u32[]{:S(2)}) collective-permute-start(bf16[32,4224]{1,0:T(8,128)(2,1)S(1)} %pad_maximum_fusion.8), channel_id=1, source_target_pairs={{0,16},{1,17},{2,18},{3,19},{4,20},{5,21},{6,22},{7,23},{8,24},{9,... | collective-permute-start | bytes 811016 | tf_op jit(solution)/shard_map/ppermute | solution.py:35
  219.5 2.1 collective-permute-done.29
  223.5 2.2 collective-permute-done.20
  226.8 2.9 %collective-permute-done.22 = bf16[32,4224]{1,0:T(8,128)(2,1)S(1)} collective-permute-done((bf16[32,4224]{1,0:T(8,128)(2,1)S(1)}, bf16[32,4224]{1,0:T(8,128)(2,1)S(1)}, u32[]{:S(2)}, u32[]{:S(2)}) %collective-permute-start.22) | collective-permute-done | bytes 270368 | tf_op jit(solution)/shard_map/ppermute | solution.py:35
  231.5 2.7 %collective-permute-start.33 = (bf16[64,1152]{1,0:T(8,128)(2,1)S(1)}, bf16[64,1152]{1,0:T(8,128)(2,1)S(1)}, u32[]{:S(2)}, u32[]{:S(2)}) collective-permute-start(bf16[64,1152]{1,0:T(8,128)(2,1)S(1)} %get-tuple-element.64), channel_id=1, source_target_pairs={{0,4},{1,5},{2,6},{3,7},{4,0},{5,1},{6,2},{7,3},{8,12},{9,13},{10,... | collective-permute-start | bytes 442376 | tf_op jit(solution)/shard_map/ppermute | solution.py:27
  237.1 3.5 %collective-permute-done.33 = bf16[64,1152]{1,0:T(8,128)(2,1)S(1)} collective-permute-done((bf16[64,1152]{1,0:T(8,128)(2,1)S(1)}, bf16[64,1152]{1,0:T(8,128)(2,1)S(1)}, u32[]{:S(2)}, u32[]{:S(2)}) %collective-permute-start.33) | collective-permute-done | bytes 147488 | tf_op jit(solution)/shard_map/ppermute | solution.py:27
  (150 shorter events, 65.9 us)
Async XLA Ops:
  6.5 100.4 %all-gather.3.cloned.1.call-start = ((), (), s32[]{:S(2)}) async-start(), calls=%async_computation | async-start | bytes 16908288 | tf_op jit(solution)/shard_map/all_gather | solution.py:223
  7.3 7.9 %collective-permute-start = (bf16[2,64,1024]{2,1,0:T(8,128)(2,1)}, bf16[2,64,1024]{2,1,0:T(8,128)(2,1)S(1)}, u32[]{:S(2)}, u32[]{:S(2)}) collective-permute-start(bf16[2,64,1024]{2,1,0:T(8,128)(2,1)} %param.21), channel_id=1, source_target_pairs={{0,32},{1,97},{2,34},{3,99},{4,36},{5,101},{6,38},{7,103},{8,40},{... | collective-permute-start | bytes 786440 | tf_op jit(solution)/shard_map/ppermute | solution.py:35
  22.7 8.0 %collective-permute-start.2 = (bf16[2,64,1024]{2,1,0:T(8,128)(2,1)S(1)}, bf16[2,64,1024]{2,1,0:T(8,128)(2,1)S(1)}, u32[]{:S(2)}, u32[]{:S(2)}) collective-permute-start(bf16[2,64,1024]{2,1,0:T(8,128)(2,1)S(1)} %collective-permute-done.1), channel_id=1, source_target_pairs={{0,32},{1,97},{2,34},{3,99},{4,36},{5,101},{6,38},{7,103},{8,40},{... | collective-permute-start | bytes 786440 | tf_op jit(solution)/shard_map/ppermute | solution.py:35
  32.8 18.5 %collective-permute-start.3 = (bf16[4,2,64,1024]{3,2,1,0:T(8,128)(2,1)S(1)}, bf16[4,2,64,1024]{3,2,1,0:T(8,128)(2,1)S(1)}, u32[]{:S(2)}, u32[]{:S(2)}) collective-permute-start(bf16[4,2,64,1024]{3,2,1,0:T(8,128)(2,1)S(1)} %get-tuple-element.57), channel_id=1, source_target_pairs={{0,8},{1,25},{2,10},{3,27},{4,12},{5,29},{6,14},{7,31},{8,16},{9,1... | collective-permute-start | bytes 3145736 | tf_op jit(solution)/shard_map/ppermute | solution.py:35
  51.4 29.5 %collective-permute-start.4 = (bf16[4,2,64,1024]{3,2,1,0:T(8,128)(2,1)S(1)}, bf16[4,2,64,1024]{3,2,1,0:T(8,128)(2,1)}, u32[]{:S(2)}, u32[]{:S(2)}) collective-permute-start(bf16[4,2,64,1024]{3,2,1,0:T(8,128)(2,1)S(1)} %collective-permute-done.3), channel_id=1, source_target_pairs={{0,8},{1,25},{2,10},{3,27},{4,12},{5,29},{6,14},{7,31},{8,16},{9,1... | collective-permute-start | bytes 3145736 | tf_op jit(solution)/shard_map/ppermute | solution.py:35
  80.9 22.5 %collective-permute-start.5 = (bf16[4,2,64,1024]{3,2,1,0:T(8,128)(2,1)}, bf16[4,2,64,1024]{3,2,1,0:T(8,128)(2,1)}, u32[]{:S(2)}, u32[]{:S(2)}) collective-permute-start(bf16[4,2,64,1024]{3,2,1,0:T(8,128)(2,1)} %collective-permute-done.4), channel_id=1, source_target_pairs={{0,8},{1,25},{2,10},{3,27},{4,12},{5,29},{6,14},{7,31},{8,16},{9,1... | collective-permute-start | bytes 3145736 | tf_op jit(solution)/shard_map/ppermute | solution.py:35
  117.1 13.7 %collective-permute-start.6 = (bf16[160,128]{1,0:T(8,128)(2,1)}, bf16[160,128]{1,0:T(8,128)(2,1)S(1)}, u32[]{:S(2)}, u32[]{:S(2)}) collective-permute-start(bf16[160,128]{1,0:T(8,128)(2,1)} %bitcast.420), channel_id=1, source_target_pairs={{0,96},{1,97},{2,98},{3,99},{4,100},{5,101},{6,102},{7,103},{8,104... | collective-permute-start | bytes 122888 | tf_op jit(solution)/shard_map/ppermute | solution.py:27
  119.8 11.0 %collective-permute-start.7 = (bf16[160,128]{1,0:T(8,128)(2,1)}, bf16[160,128]{1,0:T(8,128)(2,1)S(1)}, u32[]{:S(2)}, u32[]{:S(2)}) collective-permute-start(bf16[160,128]{1,0:T(8,128)(2,1)} %bitcast.421), channel_id=1, source_target_pairs={{0,64},{1,65},{2,66},{3,67},{4,68},{5,69},{6,70},{7,71},{8,72},{9,... | collective-permute-start | bytes 122888 | tf_op jit(solution)/shard_map/ppermute | solution.py:27
  120.6 10.3 %collective-permute-start.8 = (bf16[160,128]{1,0:T(8,128)(2,1)}, bf16[160,128]{1,0:T(8,128)(2,1)S(1)}, u32[]{:S(2)}, u32[]{:S(2)}) collective-permute-start(bf16[160,128]{1,0:T(8,128)(2,1)} %bitcast.422), channel_id=1, source_target_pairs={{0,32},{1,33},{2,34},{3,35},{4,36},{5,37},{6,38},{7,39},{8,40},{9,... | collective-permute-start | bytes 122888 | tf_op jit(solution)/shard_map/ppermute | solution.py:27
  130.9 12.4 %collective-permute-start.9 = (bf16[4,160,128]{2,1,0:T(8,128)(2,1)S(1)}, bf16[4,160,128]{2,1,0:T(8,128)(2,1)S(1)}, u32[]{:S(2)}, u32[]{:S(2)}) collective-permute-start(bf16[4,160,128]{2,1,0:T(8,128)(2,1)S(1)} %get-tuple-element.62), channel_id=1, source_target_pairs={{0,24},{1,25},{2,26},{3,27},{4,28},{5,29},{6,30},{7,31},{8,0},{9,1... | collective-permute-start | bytes 491528 | tf_op jit(solution)/shard_map/ppermute | solution.py:27
  131.7 11.6 %collective-permute-start.10 = (bf16[4,160,128]{2,1,0:T(8,128)(2,1)S(1)}, bf16[4,160,128]{2,1,0:T(8,128)(2,1)S(1)}, u32[]{:S(2)}, u32[]{:S(2)}) collective-permute-start(bf16[4,160,128]{2,1,0:T(8,128)(2,1)S(1)} %get-tuple-element.62), channel_id=1, source_target_pairs={{0,16},{1,17},{2,18},{3,19},{4,20},{5,21},{6,22},{7,23},{8,24},{9,... | collective-permute-start | bytes 491528 | tf_op jit(solution)/shard_map/ppermute | solution.py:27
  132.1 11.2 %collective-permute-start.11 = (bf16[4,160,128]{2,1,0:T(8,128)(2,1)S(1)}, bf16[4,160,128]{2,1,0:T(8,128)(2,1)S(1)}, u32[]{:S(2)}, u32[]{:S(2)}) collective-permute-start(bf16[4,160,128]{2,1,0:T(8,128)(2,1)S(1)} %get-tuple-element.62), channel_id=1, source_target_pairs={{0,8},{1,9},{2,10},{3,11},{4,12},{5,13},{6,14},{7,15},{8,16},{9,17... | collective-permute-start | bytes 491528 | tf_op jit(solution)/shard_map/ppermute | solution.py:27
  165.1 10.8 %collective-permute-start.13 = (bf16[768,4224]{1,0:T(8,128)(2,1)}, bf16[768,4224]{1,0:T(8,128)(2,1)S(1)}, u32[]{:S(2)}, u32[]{:S(2)}) collective-permute-start(bf16[768,4224]{1,0:T(8,128)(2,1)} %convolution_convert_fusion), channel_id=1, source_target_pairs={{0,1},{1,0},{2,3},{3,2},{4,5},{5,4},{6,7},{7,6},{8,9},{9,8},{10,11... | collective-permute-start | bytes 19464200 | tf_op jit(solution)/shard_map/ppermute | solution.py:27
  167.3 10.5 %collective-permute-start.14 = (bf16[128,2048]{1,0:T(8,128)(2,1)S(1)}, bf16[128,2048]{1,0:T(8,128)(2,1)S(1)}, u32[]{:S(2)}, u32[]{:S(2)}) collective-permute-start(bf16[128,2048]{1,0:T(8,128)(2,1)S(1)} %fusion.3), channel_id=1, source_target_pairs={{0,8},{1,25},{2,10},{3,27},{4,12},{5,29},{6,14},{7,31},{8,16},{9,1... | collective-permute-start | bytes 1572872 | tf_op jit(solution)/shard_map/ppermute | solution.py:35
  169.5 10.4 %collective-permute-start.23 = (bf16[128,2048]{1,0:T(8,128)(2,1)S(1)}, bf16[128,2048]{1,0:T(8,128)(2,1)S(1)}, u32[]{:S(2)}, u32[]{:S(2)}) collective-permute-start(bf16[128,2048]{1,0:T(8,128)(2,1)S(1)} %fusion.4), channel_id=1, source_target_pairs={{0,32},{1,97},{2,34},{3,99},{4,36},{5,101},{6,38},{7,103},{8,40},{... | collective-permute-start | bytes 1572872 | tf_op jit(solution)/shard_map/ppermute | solution.py:35
  171.3 12.4 %collective-permute-start.17 = (bf16[128,2176]{1,0:T(8,128)(2,1)S(1)}, bf16[128,2176]{1,0:T(8,128)(2,1)S(1)}, u32[]{:S(2)}, u32[]{:S(2)}) collective-permute-start(bf16[128,2176]{1,0:T(8,128)(2,1)S(1)} %fusion.1), channel_id=1, source_target_pairs={{0,8},{1,25},{2,10},{3,27},{4,12},{5,29},{6,14},{7,31},{8,16},{9,1... | collective-permute-start | bytes 1671176 | tf_op jit(solution)/shard_map/ppermute | solution.py:35
  173.2 12.6 %collective-permute-start.26 = (bf16[128,2176]{1,0:T(8,128)(2,1)S(1)}, bf16[128,2176]{1,0:T(8,128)(2,1)S(1)}, u32[]{:S(2)}, u32[]{:S(2)}) collective-permute-start(bf16[128,2176]{1,0:T(8,128)(2,1)S(1)} %fusion.2), channel_id=1, source_target_pairs={{0,32},{1,97},{2,34},{3,99},{4,36},{5,101},{6,38},{7,103},{8,40},{... | collective-permute-start | bytes 1671176 | tf_op jit(solution)/shard_map/ppermute | solution.py:35
  178.1 11.2 %collective-permute-start.15 = (bf16[128,2048]{1,0:T(8,128)(2,1)S(1)}, bf16[128,2048]{1,0:T(8,128)(2,1)S(1)}, u32[]{:S(2)}, u32[]{:S(2)}) collective-permute-start(bf16[128,2048]{1,0:T(8,128)(2,1)S(1)} %fusion.22), channel_id=1, source_target_pairs={{0,8},{1,25},{2,10},{3,27},{4,12},{5,29},{6,14},{7,31},{8,16},{9,1... | collective-permute-start | bytes 1572872 | tf_op jit(solution)/shard_map/ppermute | solution.py:35
  180.2 11.2 %collective-permute-start.24 = (bf16[128,2048]{1,0:T(8,128)(2,1)S(1)}, bf16[128,2048]{1,0:T(8,128)(2,1)S(1)}, u32[]{:S(2)}, u32[]{:S(2)}) collective-permute-start(bf16[128,2048]{1,0:T(8,128)(2,1)S(1)} %fusion.18), channel_id=1, source_target_pairs={{0,32},{1,97},{2,34},{3,99},{4,36},{5,101},{6,38},{7,103},{8,40},{... | collective-permute-start | bytes 1572872 | tf_op jit(solution)/shard_map/ppermute | solution.py:35
  184.2 11.1 %collective-permute-start.18 = (bf16[128,2176]{1,0:T(8,128)(2,1)S(1)}, bf16[128,2176]{1,0:T(8,128)(2,1)S(1)}, u32[]{:S(2)}, u32[]{:S(2)}) collective-permute-start(bf16[128,2176]{1,0:T(8,128)(2,1)S(1)} %fusion.13), channel_id=1, source_target_pairs={{0,8},{1,25},{2,10},{3,27},{4,12},{5,29},{6,14},{7,31},{8,16},{9,1... | collective-permute-start | bytes 1671176 | tf_op jit(solution)/shard_map/ppermute | solution.py:35
  186.3 11.1 %collective-permute-start.27 = (bf16[128,2176]{1,0:T(8,128)(2,1)S(1)}, bf16[128,2176]{1,0:T(8,128)(2,1)S(1)}, u32[]{:S(2)}, u32[]{:S(2)}) collective-permute-start(bf16[128,2176]{1,0:T(8,128)(2,1)S(1)} %fusion.9), channel_id=1, source_target_pairs={{0,32},{1,97},{2,34},{3,99},{4,36},{5,101},{6,38},{7,103},{8,40},{... | collective-permute-start | bytes 1671176 | tf_op jit(solution)/shard_map/ppermute | solution.py:35
  191.9 11.2 %collective-permute-start.25 = (bf16[128,2048]{1,0:T(8,128)(2,1)S(1)}, bf16[128,2048]{1,0:T(8,128)(2,1)S(1)}, u32[]{:S(2)}, u32[]{:S(2)}) collective-permute-start(bf16[128,2048]{1,0:T(8,128)(2,1)S(1)} %get-tuple-element.52), channel_id=1, source_target_pairs={{0,32},{1,97},{2,34},{3,99},{4,36},{5,101},{6,38},{7,103},{8,40},{... | collective-permute-start | bytes 1572872 | tf_op jit(solution)/shard_map/ppermute | solution.py:35
  192.5 11.4 %collective-permute-start.16 = (bf16[128,2048]{1,0:T(8,128)(2,1)S(1)}, bf16[128,2048]{1,0:T(8,128)(2,1)S(1)}, u32[]{:S(2)}, u32[]{:S(2)}) collective-permute-start(bf16[128,2048]{1,0:T(8,128)(2,1)S(1)} %get-tuple-element.53), channel_id=1, source_target_pairs={{0,8},{1,25},{2,10},{3,27},{4,12},{5,29},{6,14},{7,31},{8,16},{9,1... | collective-permute-start | bytes 1572872 | tf_op jit(solution)/shard_map/ppermute | solution.py:35
  197.8 11.3 %collective-permute-start.28 = (bf16[128,2176]{1,0:T(8,128)(2,1)S(1)}, bf16[128,2176]{1,0:T(8,128)(2,1)S(1)}, u32[]{:S(2)}, u32[]{:S(2)}) collective-permute-start(bf16[128,2176]{1,0:T(8,128)(2,1)S(1)} %get-tuple-element.54), channel_id=1, source_target_pairs={{0,32},{1,97},{2,34},{3,99},{4,36},{5,101},{6,38},{7,103},{8,40},{... | collective-permute-start | bytes 1671176 | tf_op jit(solution)/shard_map/ppermute | solution.py:35
  198.4 16.1 %collective-permute-start.19 = (bf16[128,2176]{1,0:T(8,128)(2,1)S(1)}, bf16[128,2176]{1,0:T(8,128)(2,1)S(1)}, u32[]{:S(2)}, u32[]{:S(2)}) collective-permute-start(bf16[128,2176]{1,0:T(8,128)(2,1)S(1)} %get-tuple-element.55), channel_id=1, source_target_pairs={{0,8},{1,25},{2,10},{3,27},{4,12},{5,29},{6,14},{7,31},{8,16},{9,1... | collective-permute-start | bytes 1671176 | tf_op jit(solution)/shard_map/ppermute | solution.py:35
  209.5 12.2 %collective-permute-start.29 = (bf16[32,4224]{1,0:T(8,128)(2,1)S(1)}, bf16[32,4224]{1,0:T(8,128)(2,1)S(1)}, u32[]{:S(2)}, u32[]{:S(2)}) collective-permute-start(bf16[32,4224]{1,0:T(8,128)(2,1)S(1)} %pad_maximum_fusion.7), channel_id=1, source_target_pairs={{0,24},{1,9},{2,26},{3,11},{4,28},{5,13},{6,30},{7,15},{8,0},{9,17... | collective-permute-start | bytes 811016 | tf_op jit(solution)/shard_map/ppermute | solution.py:35
  211.3 10.3 %collective-permute-start.30 = (bf16[32,4224]{1,0:T(8,128)(2,1)S(1)}, bf16[32,4224]{1,0:T(8,128)(2,1)S(1)}, u32[]{:S(2)}, u32[]{:S(2)}) collective-permute-start(bf16[32,4224]{1,0:T(8,128)(2,1)S(1)} %pad_maximum_fusion.8), channel_id=1, source_target_pairs={{0,16},{1,17},{2,18},{3,19},{4,20},{5,21},{6,22},{7,23},{8,24},{9,... | collective-permute-start | bytes 811016 | tf_op jit(solution)/shard_map/ppermute | solution.py:35
  214.5 8.9 %collective-permute-start.31 = (bf16[32,4224]{1,0:T(8,128)(2,1)S(1)}, bf16[32,4224]{1,0:T(8,128)(2,1)S(1)}, u32[]{:S(2)}, u32[]{:S(2)}) collective-permute-start(bf16[32,4224]{1,0:T(8,128)(2,1)S(1)} %pad_maximum_fusion.9), channel_id=1, source_target_pairs={{0,8},{1,25},{2,10},{3,27},{4,12},{5,29},{6,14},{7,31},{8,16},{9,1... | collective-permute-start | bytes 811016 | tf_op jit(solution)/shard_map/ppermute | solution.py:35
  215.0 10.8 %collective-permute-start.20 = (bf16[32,4224]{1,0:T(8,128)(2,1)S(1)}, bf16[32,4224]{1,0:T(8,128)(2,1)S(1)}, u32[]{:S(2)}, u32[]{:S(2)}) collective-permute-start(bf16[32,4224]{1,0:T(8,128)(2,1)S(1)} %pad_maximum_fusion.4), channel_id=1, source_target_pairs={{0,96},{1,33},{2,98},{3,35},{4,100},{5,37},{6,102},{7,39},{8,104},... | collective-permute-start | bytes 811016 | tf_op jit(solution)/shard_map/ppermute | solution.py:35
  216.6 10.2 %collective-permute-start.21 = (bf16[32,4224]{1,0:T(8,128)(2,1)S(1)}, bf16[32,4224]{1,0:T(8,128)(2,1)S(1)}, u32[]{:S(2)}, u32[]{:S(2)}) collective-permute-start(bf16[32,4224]{1,0:T(8,128)(2,1)S(1)} %pad_maximum_fusion.5), channel_id=1, source_target_pairs={{0,64},{1,65},{2,66},{3,67},{4,68},{5,69},{6,70},{7,71},{8,72},{9,... | collective-permute-start | bytes 811016 | tf_op jit(solution)/shard_map/ppermute | solution.py:35
  221.6 8.1 %collective-permute-start.22 = (bf16[32,4224]{1,0:T(8,128)(2,1)S(1)}, bf16[32,4224]{1,0:T(8,128)(2,1)S(1)}, u32[]{:S(2)}, u32[]{:S(2)}) collective-permute-start(bf16[32,4224]{1,0:T(8,128)(2,1)S(1)} %pad_maximum_fusion.6), channel_id=1, source_target_pairs={{0,32},{1,97},{2,34},{3,99},{4,36},{5,101},{6,38},{7,103},{8,40},{... | collective-permute-start | bytes 811016 | tf_op jit(solution)/shard_map/ppermute | solution.py:35
  231.5 9.1 %collective-permute-start.33 = (bf16[64,1152]{1,0:T(8,128)(2,1)S(1)}, bf16[64,1152]{1,0:T(8,128)(2,1)S(1)}, u32[]{:S(2)}, u32[]{:S(2)}) collective-permute-start(bf16[64,1152]{1,0:T(8,128)(2,1)S(1)} %get-tuple-element.64), channel_id=1, source_target_pairs={{0,4},{1,5},{2,6},{3,7},{4,0},{5,1},{6,2},{7,3},{8,12},{9,13},{10,... | collective-permute-start | bytes 442376 | tf_op jit(solution)/shard_map/ppermute | solution.py:27
  (16 other events, 128.3 us)
Sparse Core Ops, SparseCore 0:
  10.5 86.9 all-gather.2
where the time goes:
time: 250 us; the launch traced here: 249 us
  waiting for transfers between devices  85 us (34%)
  starting transfers between devices  42.6 us (17%)
  Pallas kernels  39.6 us (16%)
  matrix products  21.3 us (9%)
  blocking collectives  18.7 us (7%)
  local copies, waits for them, and re-layouts  15.5 us (6%)
  between operations  14.6 us (6%)
  other arithmetic  11.8 us (5%)
    ppermute x24, waiting for transfers between devices, onward(): return lax.ppermute(value, AXES, pairs(move))  78.3 us
    ppermute x24, starting transfers between devices, onward(): return lax.ppermute(value, AXES, pairs(move))  29.8 us
    unnamed x1, blocking collectives  18.7 us
    pallas_call x2, Pallas kernels, gate_up(): pl.pallas_call(gate_up_kernel, grid=(4,), in_specs=specs, out_specs=pl.Bl...  18.6 us
    ppermute x11, starting transfers between devices, send(): lax.ppermute(value, AXES, pairs(lambda y, z, x, c: (y + dy, z + dz, x + d...  12.8 us
    pallas_call x1, Pallas kernels, hidden_rows(): pl.pallas_call(hidden_kernel, grid_spec=pltpu.PrefetchScalarGridSpec(num_...  10.9 us
    dot_general x28, matrix products, own_part(): part = jnp.dot(h, mine[ch], preferred_element_type=F32)  10.3 us
    pallas_call x1, Pallas kernels, low_own_rows(): pl.pallas_call(low_kernel, grid=(4,), in_specs=[pl.BlockSpec((16, 2, 64,...  10.2 us
  transfers between devices with their start and end apart: 36, of which 23 were waited for; matrix products, arithmetic and copies ran while one was open for 17% of the time, Pallas kernels for 7%

commit v1 on v0

--- a/solution.py
+++ b/solution.py
@@ -228,8 +228,8 @@
         exits = [exits]
         for _ in range(3):
             exits.append(ring(exits[-1], axis))
-        exits = jnp.stack(exits)
-    exits = exits.reshape(2048, 1024)
+        if axis == "y":
+            exits, ids = lax.optimization_barrier((jnp.stack(exits), ids))
 
     names = jnp.arange(32, dtype=jnp.int32)
     member = ids[:, None] == names[None, :]
@@ -263,10 +263,12 @@
     theirs = columns(turns, 1 - c, 384, True)
     mine = (columns((1, 2), c, 256, False), columns((3, 0), c, 384, True))
 
-    every, exits, select, slot, row, theirs, mine = lax.optimization_barrier(
-        (every, exits, select, slot, (relative * 160 + row)[:, None], theirs, mine)
+    every, select, slot, row, theirs, mine = lax.optimization_barrier(
+        (every, select, slot, (relative * 160 + row)[:, None], theirs, mine)
     )
     low_own = low_own_rows(every, adapter_entry_maps, select).reshape(160, 128)
+    low_own, exits = lax.optimization_barrier((low_own, exits))
+    exits = jnp.stack(exits).reshape(2048, 1024)
     low = jnp.stack([low_own] + [send(low_own, dy=-d) for d in (1, 2, 3)])
     low = jnp.stack([low] + [send(low, dz=-d) for d in (1, 2, 3)]).reshape(2560, 128)
     sums = None

time: 250 us -> 258 us (1.032)
  waiting for transfers between devices: 85 us -> 98.5 us
  starting transfers between devices: 42.6 us -> 36.8 us
    unnamed x1 -> x0, blocking collectives: 18.7 us -> none
    optimization_barrier x0 -> x1, blocking collectives: none -> 17.7 us  [on_device(): exits, ids = lax.optimization_barrier((jnp.stack(exits), ids))]
    ppermute x24, waiting for transfers between devices: 78.3 us -> 91.6 us  [onward(): return lax.ppermute(value, AXES, pairs(move))]
    ppermute x24, starting transfers between devices: 29.8 us -> 24.4 us  [onward(): return lax.ppermute(value, AXES, pairs(move))]
  transfers between devices with their start and end apart: 36 -> 36, of which waited for: 23 -> 21; matrix products, arithmetic and copies ran while one was open for 17% -> 16% of each run, Pallas kernels for 7% -> 11%
where the time goes in v1:
time: 258 us; the launch traced here: 255 us
  waiting for transfers between devices  98.5 us (38%)
  Pallas kernels  39.6 us (15%)
  starting transfers between devices  36.8 us (14%)
  matrix products  21.2 us (8%)
  blocking collectives  17.7 us (7%)
  local copies, waits for them, and re-layouts  16.3 us (6%)
  between operations  14.7 us (6%)
  other arithmetic  10.5 us (4%)
    ppermute x24, waiting for transfers between devices, onward(): return lax.ppermute(value, AXES, pairs(move))  91.6 us
    ppermute x24, starting transfers between devices, onward(): return lax.ppermute(value, AXES, pairs(move))  24.4 us
    pallas_call x2, Pallas kernels, gate_up(): pl.pallas_call(gate_up_kernel, grid=(4,), in_specs=specs, out_specs=pl.Bl...  18.6 us
    optimization_barrier x1, blocking collectives, on_device(): exits, ids = lax.optimization_barrier((jnp.stack(exits), ids))  17.7 us
    ppermute x11, starting transfers between devices, send(): lax.ppermute(value, AXES, pairs(lambda y, z, x, c: (y + dy, z + dz, x + d...  12.4 us
    pallas_call x1, Pallas kernels, hidden_rows(): pl.pallas_call(hidden_kernel, grid_spec=pltpu.PrefetchScalarGridSpec(num_...  10.9 us
    dot_general x28, matrix products, own_part(): part = jnp.dot(h, mine[ch], preferred_element_type=F32)  10.3 us
    pallas_call x1, Pallas kernels, low_own_rows(): pl.pallas_call(low_kernel, grid=(4,), in_specs=[pl.BlockSpec((16, 2, 64,...  10.2 us
  transfers between devices with their start and end apart: 36, of which 21 were waited for; matrix products, arithmetic and copies ran while one was open for 16% of the time, Pallas kernels for 11%

profile of v1, /device:TPU:0, one launch (start us, length us, event | category | flops | bytes accessed | tf_op | source)
XLA Modules:
  0.0 255.3 jit_solution(514370388317978245)
XLA Ops:
  9.0 6.1 %collective-permute-done = bf16[2,64,1024]{2,1,0:T(8,128)(2,1)S(1)} collective-permute-done((bf16[2,64,1024]{2,1,0:T(8,128)(2,1)}, bf16[2,64,1024]{2,1,0:T(8,128)(2,1)S(1)}, u32[]{:S(2)}, u32[]{:S(2)}) %collective-permute-start) | collective-permute-done | bytes 262176 | tf_op jit(solution)/shard_map/ppermute | solution.py:35
  15.6 7.1 %collective-permute-done.1 = bf16[2,64,1024]{2,1,0:T(8,128)(2,1)S(1)} collective-permute-done((bf16[2,64,1024]{2,1,0:T(8,128)(2,1)S(1)}, bf16[2,64,1024]{2,1,0:T(8,128)(2,1)S(1)}, u32[]{:S(2)}, u32[]{:S(2)}) %collective-permute-start.1) | collective-permute-done | bytes 262176 | tf_op jit(solution)/shard_map/ppermute | solution.py:35
  25.5 17.7 %all-reduce.3 = s32[1024]{0:T(1024)S(1)} all-reduce(s32[1024]{0:T(1024)S(1)} %dynamic-update-slice), channel_id=1, replica_groups=mesh['adapter'=16,'tensor'=8] {'adapter'}, use_global_device_ids=true, to_apply=%add.3 | all-reduce | flops 1024 | bytes 8192 | tf_op jit(solution)/shard_map/optimization_barrier | solution.py:232
  47.3 17.0 %collective-permute-done.3 = bf16[4,2,64,1024]{3,2,1,0:T(8,128)(2,1)} collective-permute-done((bf16[4,2,64,1024]{3,2,1,0:T(8,128)(2,1)S(1)}, bf16[4,2,64,1024]{3,2,1,0:T(8,128)(2,1)}, u32[]{:S(2)}, u32[]{:S(2)}) %collective-permute-start.3) | collective-permute-done | bytes 1048608 | tf_op jit(solution)/shard_map/ppermute | solution.py:35
  66.4 2.0 dynamic-slice_dynamic-update-slice_fusion.5
  68.4 2.2 dynamic-slice_dynamic-update-slice_fusion.1
  71.4 2.2 dynamic-slice_dynamic-update-slice_fusion
  74.2 28.2 %collective-permute-done.4 = bf16[4,2,64,1024]{3,2,1,0:T(8,128)(2,1)} collective-permute-done((bf16[4,2,64,1024]{3,2,1,0:T(8,128)(2,1)}, bf16[4,2,64,1024]{3,2,1,0:T(8,128)(2,1)}, u32[]{:S(2)}, u32[]{:S(2)}) %collective-permute-start.4) | collective-permute-done | bytes 1048608 | tf_op jit(solution)/shard_map/ppermute | solution.py:35
  104.5 3.2 %fusion.34.row_ref = s32[1024,1]{1,0:T(8,128)} fusion(s32[1024,1]{1,0:T(8,128)S(1)} %copy.23, s32[1024,1]{1,0:T(8,128)} %copy.19, s32[]{:T(128)S(6)} %select_n.243, s32[]{:T(128)S(6)} %select_n.245), kind=kLoop, calls=%fused_computation.82 | loop fusion | flops 69632 | bytes 12296 | tf_op jit(solution)/shard_map/add | solution.py:267
  107.8 10.2 %low_own.1 = bf16[2,80,128]{2,1,0:T(8,128)(2,1)} custom-call(bf16[16,8,64,1024]{3,2,1,0:T(8,128)(2,1)} %bitcast.344, bf16[2,8192,128]{2,1,0:T(8,128)(2,1)} %e_ref.1, bf16[2,80,1024]{2,1,0:T(8,128)(2,1)} %compare_convert_fusion.s_ref), custom_call_target="tpu_custom_call" | custom-call | flops 4294967296 | bytes 22020096 | tf_op jit(solution)/shard_map/low_own/pallas_call | solution.py:74
  122.0 9.3 %gate_up.2.refs_0_ = f32[2,512,512]{2,1,0:T(8,128)} custom-call(bf16[16,8,64,1024]{3,2,1,0:T(8,128)(2,1)} %bitcast.345, bf16[224,8192]{1,0:T(8,128)(2,1)} %bitcast.348, bf16[224,8192]{1,0:T(8,128)(2,1)} %bitcast.350), custom_call_target="tpu_custom_call" | custom-call | flops 4294967296 | bytes 16777216 | tf_op jit(solution)/shard_map/gate_up/pallas_call | solution.py:119
  131.4 3.9 %collective-permute-start.10 = (bf16[4,160,128]{2,1,0:T(8,128)(2,1)S(1)}, bf16[4,160,128]{2,1,0:T(8,128)(2,1)S(1)}, u32[]{:S(2)}, u32[]{:S(2)}) collective-permute-start(bf16[4,160,128]{2,1,0:T(8,128)(2,1)S(1)} %get-tuple-element.72), channel_id=1, source_target_pairs={{0,16},{1,17},{2,18},{3,19},{4,20},{5,21},{6,22},{7,23},{8,24},{9,... | collective-permute-start | bytes 491528 | tf_op jit(solution)/shard_map/ppermute | solution.py:27
  135.4 9.3 %gate_up.3 = f32[2,512,512]{2,1,0:T(8,128)} custom-call(bf16[16,8,64,1024]{3,2,1,0:T(8,128)(2,1)} %bitcast.346, bf16[224,8192]{1,0:T(8,128)(2,1)} %bitcast.349, bf16[224,8192]{1,0:T(8,128)(2,1)} %bitcast.351, f32[2,512,512]{2,1,0:T(8,128)} %gate_up.2.refs_0_), custom_call_target="tpu_custom_call", output_to_operand_aliasing={{}: (3, {})} | custom-call | flops 4294967296 | bytes 16777216 | tf_op jit(solution)/shard_map/gate_up/pallas_call | solution.py:119
  146.6 10.9 %hidden_rows.1 = (bf16[4,2,4,32,384]{4,3,2,1,0:T(8,128)(2,1)}, bf16[4,2,4,32,384]{4,3,2,1,0:T(8,128)(2,1)}) custom-call(s32[8]{0:T(128)} %pad_add_fusion.place, f32[4,256,512]{2,1,0:T(8,128)} %bitcast.374, s32[1024,1]{1,0:T(8,128)} %copy.24.slot_ref, s32[1024,1]{1,0:T(8,128)} %fusion.34.row_ref, bf16[2560,128]{1,0:T(8,128)(2,1)} %bitcast.411, ...), custom_call_target="tpu_custom_call" | custom-call | flops 2684354560 | bytes 16777216 | tf_op jit(solution)/shard_map/hidden_rows/pallas_call | solution.py:179
  158.4 3.4 %convolution_convert_fusion.1 = bf16[256,4224]{1,0:T(8,128)(2,1)S(1)} fusion(bf16[256,384]{1,0:T(8,128)(2,1)S(1)} %bitcast.409, bf16[384,4224]{1,0:T(8,128)(2,1)} %get-tuple-element.40), kind=kOutput, calls=%fused_computation.1 | convolution fusion | flops 831553536 | bytes 5603328 | tf_op jit(solution)/shard_map/dot_general | solution.py:293
  162.0 5.5 %convolution_convert_fusion = bf16[768,4224]{1,0:T(8,128)(2,1)} fusion(bf16[768,384]{1,0:T(8,128)(2,1)S(1)} %bitcast.412, bf16[384,4224]{1,0:T(8,128)(2,1)S(1)} %copy-done), kind=kOutput, calls=%fused_computation | convolution fusion | flops 2494660608 | bytes 10321920 | tf_op jit(solution)/shard_map/dot_general | solution.py:295
  170.6 2.0 collective-permute-start.17
  172.6 2.0 collective-permute-start.23
  178.7 7.5 %collective-permute-done.23 = bf16[128,2048]{1,0:T(8,128)(2,1)S(1)} collective-permute-done((bf16[128,2048]{1,0:T(8,128)(2,1)S(1)}, bf16[128,2048]{1,0:T(8,128)(2,1)S(1)}, u32[]{:S(2)}, u32[]{:S(2)}) %collective-permute-start.23) | collective-permute-done | bytes 524320 | tf_op jit(solution)/shard_map/ppermute | solution.py:35
  187.3 1.9 collective-permute-start.15
  192.2 5.0 %collective-permute-done.24 = bf16[128,2048]{1,0:T(8,128)(2,1)S(1)} collective-permute-done((bf16[128,2048]{1,0:T(8,128)(2,1)S(1)}, bf16[128,2048]{1,0:T(8,128)(2,1)S(1)}, u32[]{:S(2)}, u32[]{:S(2)}) %collective-permute-start.24) | collective-permute-done | bytes 524320 | tf_op jit(solution)/shard_map/ppermute | solution.py:35
  200.5 2.6 %collective-permute-done.27 = bf16[128,2176]{1,0:T(8,128)(2,1)S(1)} collective-permute-done((bf16[128,2176]{1,0:T(8,128)(2,1)S(1)}, bf16[128,2176]{1,0:T(8,128)(2,1)S(1)}, u32[]{:S(2)}, u32[]{:S(2)}) %collective-permute-start.27) | collective-permute-done | bytes 557088 | tf_op jit(solution)/shard_map/ppermute | solution.py:35
  206.4 3.0 %collective-permute-done.16 = bf16[128,2048]{1,0:T(8,128)(2,1)S(1)} collective-permute-done((bf16[128,2048]{1,0:T(8,128)(2,1)S(1)}, bf16[128,2048]{1,0:T(8,128)(2,1)S(1)}, u32[]{:S(2)}, u32[]{:S(2)}) %collective-permute-start.16) | collective-permute-done | bytes 524320 | tf_op jit(solution)/shard_map/ppermute | solution.py:35
  211.8 3.6 %collective-permute-done.19 = bf16[128,2176]{1,0:T(8,128)(2,1)S(1)} collective-permute-done((bf16[128,2176]{1,0:T(8,128)(2,1)S(1)}, bf16[128,2176]{1,0:T(8,128)(2,1)S(1)}, u32[]{:S(2)}, u32[]{:S(2)}) %collective-permute-start.19) | collective-permute-done | bytes 557088 | tf_op jit(solution)/shard_map/ppermute | solution.py:35
  215.8 2.1 collective-permute-start.22
  218.3 2.6 collective-permute-start.21
  225.3 3.1 %collective-permute-done.22 = bf16[32,4224]{1,0:T(8,128)(2,1)S(1)} collective-permute-done((bf16[32,4224]{1,0:T(8,128)(2,1)S(1)}, bf16[32,4224]{1,0:T(8,128)(2,1)S(1)}, u32[]{:S(2)}, u32[]{:S(2)}) %collective-permute-start.22) | collective-permute-done | bytes 270368 | tf_op jit(solution)/shard_map/ppermute | solution.py:35
  229.0 2.0 collective-permute-done.21
  231.1 3.5 %collective-permute-done.31 = bf16[32,4224]{1,0:T(8,128)(2,1)S(1)} collective-permute-done((bf16[32,4224]{1,0:T(8,128)(2,1)S(1)}, bf16[32,4224]{1,0:T(8,128)(2,1)S(1)}, u32[]{:S(2)}, u32[]{:S(2)}) %collective-permute-start.31) | collective-permute-done | bytes 270368 | tf_op jit(solution)/shard_map/ppermute | solution.py:35
  235.7 2.8 %collective-permute-start.34 = (bf16[64,1152]{1,0:T(8,128)(2,1)S(1)}, bf16[64,1152]{1,0:T(8,128)(2,1)S(1)}, u32[]{:S(2)}, u32[]{:S(2)}) collective-permute-start(bf16[64,1152]{1,0:T(8,128)(2,1)S(1)} %get-tuple-element.75), channel_id=1, source_target_pairs={{0,6},{1,7},{2,0},{3,1},{4,2},{5,3},{6,4},{7,5},{8,14},{9,15},{10,... | collective-permute-start | bytes 442376 | tf_op jit(solution)/shard_map/ppermute | solution.py:27
  240.3 2.1 pad_maximum_fusion
  242.8 2.5 collective-permute-done.33
  (142 shorter events, 54.2 us)
Async XLA Ops:
  6.5 101.3 %all-gather.3.cloned.1.call-start = ((), (), s32[]{:S(2)}) async-start(), calls=%async_computation | async-start | bytes 16908288 | tf_op jit(solution)/shard_map/all_gather | solution.py:223
  7.3 7.9 %collective-permute-start = (bf16[2,64,1024]{2,1,0:T(8,128)(2,1)}, bf16[2,64,1024]{2,1,0:T(8,128)(2,1)S(1)}, u32[]{:S(2)}, u32[]{:S(2)}) collective-permute-start(bf16[2,64,1024]{2,1,0:T(8,128)(2,1)} %param.21), channel_id=1, source_target_pairs={{0,32},{1,97},{2,34},{3,99},{4,36},{5,101},{6,38},{7,103},{8,40},{... | collective-permute-start | bytes 786440 | tf_op jit(solution)/shard_map/ppermute | solution.py:35
  15.1 7.6 %collective-permute-start.1 = (bf16[2,64,1024]{2,1,0:T(8,128)(2,1)S(1)}, bf16[2,64,1024]{2,1,0:T(8,128)(2,1)S(1)}, u32[]{:S(2)}, u32[]{:S(2)}) collective-permute-start(bf16[2,64,1024]{2,1,0:T(8,128)(2,1)S(1)} %collective-permute-done), channel_id=1, source_target_pairs={{0,32},{1,97},{2,34},{3,99},{4,36},{5,101},{6,38},{7,103},{8,40},{... | collective-permute-start | bytes 786440 | tf_op jit(solution)/shard_map/ppermute | solution.py:35
  22.7 20.5 %collective-permute-start.2 = (bf16[2,64,1024]{2,1,0:T(8,128)(2,1)S(1)}, bf16[2,64,1024]{2,1,0:T(8,128)(2,1)S(1)}, u32[]{:S(2)}, u32[]{:S(2)}) collective-permute-start(bf16[2,64,1024]{2,1,0:T(8,128)(2,1)S(1)} %collective-permute-done.1), channel_id=1, source_target_pairs={{0,32},{1,97},{2,34},{3,99},{4,36},{5,101},{6,38},{7,103},{8,40},{... | collective-permute-start | bytes 786440 | tf_op jit(solution)/shard_map/ppermute | solution.py:35
  44.3 20.0 %collective-permute-start.3 = (bf16[4,2,64,1024]{3,2,1,0:T(8,128)(2,1)S(1)}, bf16[4,2,64,1024]{3,2,1,0:T(8,128)(2,1)}, u32[]{:S(2)}, u32[]{:S(2)}) collective-permute-start(bf16[4,2,64,1024]{3,2,1,0:T(8,128)(2,1)S(1)} %pad_maximum_fusion.2), channel_id=1, source_target_pairs={{0,8},{1,25},{2,10},{3,27},{4,12},{5,29},{6,14},{7,31},{8,16},{9,1... | collective-permute-start | bytes 3145736 | tf_op jit(solution)/shard_map/ppermute | solution.py:35
  64.3 38.1 %collective-permute-start.4 = (bf16[4,2,64,1024]{3,2,1,0:T(8,128)(2,1)}, bf16[4,2,64,1024]{3,2,1,0:T(8,128)(2,1)}, u32[]{:S(2)}, u32[]{:S(2)}) collective-permute-start(bf16[4,2,64,1024]{3,2,1,0:T(8,128)(2,1)} %collective-permute-done.3), channel_id=1, source_target_pairs={{0,8},{1,25},{2,10},{3,27},{4,12},{5,29},{6,14},{7,31},{8,16},{9,1... | collective-permute-start | bytes 3145736 | tf_op jit(solution)/shard_map/ppermute | solution.py:35
  102.4 16.3 %collective-permute-start.5 = (bf16[4,2,64,1024]{3,2,1,0:T(8,128)(2,1)}, bf16[4,2,64,1024]{3,2,1,0:T(8,128)(2,1)}, u32[]{:S(2)}, u32[]{:S(2)}) collective-permute-start(bf16[4,2,64,1024]{3,2,1,0:T(8,128)(2,1)} %collective-permute-done.4), channel_id=1, source_target_pairs={{0,8},{1,25},{2,10},{3,27},{4,12},{5,29},{6,14},{7,31},{8,16},{9,1... | collective-permute-start | bytes 3145736 | tf_op jit(solution)/shard_map/ppermute | solution.py:35
  118.7 12.5 %collective-permute-start.8 = (bf16[160,128]{1,0:T(8,128)(2,1)}, bf16[160,128]{1,0:T(8,128)(2,1)S(1)}, u32[]{:S(2)}, u32[]{:S(2)}) collective-permute-start(bf16[160,128]{1,0:T(8,128)(2,1)} %bitcast.417), channel_id=1, source_target_pairs={{0,32},{1,33},{2,34},{3,35},{4,36},{5,37},{6,38},{7,39},{8,40},{9,... | collective-permute-start | bytes 122888 | tf_op jit(solution)/shard_map/ppermute | solution.py:27
  118.7 12.5 %collective-permute-start.7 = (bf16[160,128]{1,0:T(8,128)(2,1)}, bf16[160,128]{1,0:T(8,128)(2,1)S(1)}, u32[]{:S(2)}, u32[]{:S(2)}) collective-permute-start(bf16[160,128]{1,0:T(8,128)(2,1)} %bitcast.418), channel_id=1, source_target_pairs={{0,64},{1,65},{2,66},{3,67},{4,68},{5,69},{6,70},{7,71},{8,72},{9,... | collective-permute-start | bytes 122888 | tf_op jit(solution)/shard_map/ppermute | solution.py:27
  120.1 11.2 %collective-permute-start.6 = (bf16[160,128]{1,0:T(8,128)(2,1)}, bf16[160,128]{1,0:T(8,128)(2,1)S(1)}, u32[]{:S(2)}, u32[]{:S(2)}) collective-permute-start(bf16[160,128]{1,0:T(8,128)(2,1)} %bitcast.419), channel_id=1, source_target_pairs={{0,96},{1,97},{2,98},{3,99},{4,100},{5,101},{6,102},{7,103},{8,104... | collective-permute-start | bytes 122888 | tf_op jit(solution)/shard_map/ppermute | solution.py:27
  131.3 14.3 %collective-permute-start.11 = (bf16[4,160,128]{2,1,0:T(8,128)(2,1)S(1)}, bf16[4,160,128]{2,1,0:T(8,128)(2,1)S(1)}, u32[]{:S(2)}, u32[]{:S(2)}) collective-permute-start(bf16[4,160,128]{2,1,0:T(8,128)(2,1)S(1)} %get-tuple-element.72), channel_id=1, source_target_pairs={{0,8},{1,9},{2,10},{3,11},{4,12},{5,13},{6,14},{7,15},{8,16},{9,17... | collective-permute-start | bytes 491528 | tf_op jit(solution)/shard_map/ppermute | solution.py:27
  131.4 14.3 %collective-permute-start.10 = (bf16[4,160,128]{2,1,0:T(8,128)(2,1)S(1)}, bf16[4,160,128]{2,1,0:T(8,128)(2,1)S(1)}, u32[]{:S(2)}, u32[]{:S(2)}) collective-permute-start(bf16[4,160,128]{2,1,0:T(8,128)(2,1)S(1)} %get-tuple-element.72), channel_id=1, source_target_pairs={{0,16},{1,17},{2,18},{3,19},{4,20},{5,21},{6,22},{7,23},{8,24},{9,... | collective-permute-start | bytes 491528 | tf_op jit(solution)/shard_map/ppermute | solution.py:27
  135.3 10.3 %collective-permute-start.9 = (bf16[4,160,128]{2,1,0:T(8,128)(2,1)S(1)}, bf16[4,160,128]{2,1,0:T(8,128)(2,1)S(1)}, u32[]{:S(2)}, u32[]{:S(2)}) collective-permute-start(bf16[4,160,128]{2,1,0:T(8,128)(2,1)S(1)} %get-tuple-element.72), channel_id=1, source_target_pairs={{0,24},{1,25},{2,26},{3,27},{4,28},{5,29},{6,30},{7,31},{8,0},{9,1... | collective-permute-start | bytes 491528 | tf_op jit(solution)/shard_map/ppermute | solution.py:27
  167.5 10.8 %collective-permute-start.13 = (bf16[768,4224]{1,0:T(8,128)(2,1)}, bf16[768,4224]{1,0:T(8,128)(2,1)S(1)}, u32[]{:S(2)}, u32[]{:S(2)}) collective-permute-start(bf16[768,4224]{1,0:T(8,128)(2,1)} %convolution_convert_fusion), channel_id=1, source_target_pairs={{0,1},{1,0},{2,3},{3,2},{4,5},{5,4},{6,7},{7,6},{8,9},{9,8},{10,11... | collective-permute-start | bytes 19464200 | tf_op jit(solution)/shard_map/ppermute | solution.py:27
  169.7 19.5 %collective-permute-start.26 = (bf16[128,2176]{1,0:T(8,128)(2,1)S(1)}, bf16[128,2176]{1,0:T(8,128)(2,1)S(1)}, u32[]{:S(2)}, u32[]{:S(2)}) collective-permute-start(bf16[128,2176]{1,0:T(8,128)(2,1)S(1)} %fusion.2), channel_id=1, source_target_pairs={{0,32},{1,97},{2,34},{3,99},{4,36},{5,101},{6,38},{7,103},{8,40},{... | collective-permute-start | bytes 1671176 | tf_op jit(solution)/shard_map/ppermute | solution.py:35
  170.6 20.8 %collective-permute-start.17 = (bf16[128,2176]{1,0:T(8,128)(2,1)S(1)}, bf16[128,2176]{1,0:T(8,128)(2,1)S(1)}, u32[]{:S(2)}, u32[]{:S(2)}) collective-permute-start(bf16[128,2176]{1,0:T(8,128)(2,1)S(1)} %fusion.1), channel_id=1, source_target_pairs={{0,8},{1,25},{2,10},{3,27},{4,12},{5,29},{6,14},{7,31},{8,16},{9,1... | collective-permute-start | bytes 1671176 | tf_op jit(solution)/shard_map/ppermute | solution.py:35
  172.6 13.5 %collective-permute-start.23 = (bf16[128,2048]{1,0:T(8,128)(2,1)S(1)}, bf16[128,2048]{1,0:T(8,128)(2,1)S(1)}, u32[]{:S(2)}, u32[]{:S(2)}) collective-permute-start(bf16[128,2048]{1,0:T(8,128)(2,1)S(1)} %fusion.4), channel_id=1, source_target_pairs={{0,32},{1,97},{2,34},{3,99},{4,36},{5,101},{6,38},{7,103},{8,40},{... | collective-permute-start | bytes 1572872 | tf_op jit(solution)/shard_map/ppermute | solution.py:35
  174.7 12.3 %collective-permute-start.14 = (bf16[128,2048]{1,0:T(8,128)(2,1)S(1)}, bf16[128,2048]{1,0:T(8,128)(2,1)S(1)}, u32[]{:S(2)}, u32[]{:S(2)}) collective-permute-start(bf16[128,2048]{1,0:T(8,128)(2,1)S(1)} %fusion.3), channel_id=1, source_target_pairs={{0,8},{1,25},{2,10},{3,27},{4,12},{5,29},{6,14},{7,31},{8,16},{9,1... | collective-permute-start | bytes 1572872 | tf_op jit(solution)/shard_map/ppermute | solution.py:35
  186.5 10.7 %collective-permute-start.24 = (bf16[128,2048]{1,0:T(8,128)(2,1)S(1)}, bf16[128,2048]{1,0:T(8,128)(2,1)S(1)}, u32[]{:S(2)}, u32[]{:S(2)}) collective-permute-start(bf16[128,2048]{1,0:T(8,128)(2,1)S(1)} %fusion.18), channel_id=1, source_target_pairs={{0,32},{1,97},{2,34},{3,99},{4,36},{5,101},{6,38},{7,103},{8,40},{... | collective-permute-start | bytes 1572872 | tf_op jit(solution)/shard_map/ppermute | solution.py:35
  187.3 10.5 %collective-permute-start.15 = (bf16[128,2048]{1,0:T(8,128)(2,1)S(1)}, bf16[128,2048]{1,0:T(8,128)(2,1)S(1)}, u32[]{:S(2)}, u32[]{:S(2)}) collective-permute-start(bf16[128,2048]{1,0:T(8,128)(2,1)S(1)} %fusion.22), channel_id=1, source_target_pairs={{0,8},{1,25},{2,10},{3,27},{4,12},{5,29},{6,14},{7,31},{8,16},{9,1... | collective-permute-start | bytes 1572872 | tf_op jit(solution)/shard_map/ppermute | solution.py:35
  189.7 13.4 %collective-permute-start.27 = (bf16[128,2176]{1,0:T(8,128)(2,1)S(1)}, bf16[128,2176]{1,0:T(8,128)(2,1)S(1)}, u32[]{:S(2)}, u32[]{:S(2)}) collective-permute-start(bf16[128,2176]{1,0:T(8,128)(2,1)S(1)} %fusion.9), channel_id=1, source_target_pairs={{0,32},{1,97},{2,34},{3,99},{4,36},{5,101},{6,38},{7,103},{8,40},{... | collective-permute-start | bytes 1671176 | tf_op jit(solution)/shard_map/ppermute | solution.py:35
  191.9 11.8 %collective-permute-start.18 = (bf16[128,2176]{1,0:T(8,128)(2,1)S(1)}, bf16[128,2176]{1,0:T(8,128)(2,1)S(1)}, u32[]{:S(2)}, u32[]{:S(2)}) collective-permute-start(bf16[128,2176]{1,0:T(8,128)(2,1)S(1)} %fusion.13), channel_id=1, source_target_pairs={{0,8},{1,25},{2,10},{3,27},{4,12},{5,29},{6,14},{7,31},{8,16},{9,1... | collective-permute-start | bytes 1671176 | tf_op jit(solution)/shard_map/ppermute | solution.py:35
  198.2 11.2 %collective-permute-start.16 = (bf16[128,2048]{1,0:T(8,128)(2,1)S(1)}, bf16[128,2048]{1,0:T(8,128)(2,1)S(1)}, u32[]{:S(2)}, u32[]{:S(2)}) collective-permute-start(bf16[128,2048]{1,0:T(8,128)(2,1)S(1)} %get-tuple-element.65), channel_id=1, source_target_pairs={{0,8},{1,25},{2,10},{3,27},{4,12},{5,29},{6,14},{7,31},{8,16},{9,1... | collective-permute-start | bytes 1572872 | tf_op jit(solution)/shard_map/ppermute | solution.py:35
  199.7 10.6 %collective-permute-start.25 = (bf16[128,2048]{1,0:T(8,128)(2,1)S(1)}, bf16[128,2048]{1,0:T(8,128)(2,1)S(1)}, u32[]{:S(2)}, u32[]{:S(2)}) collective-permute-start(bf16[128,2048]{1,0:T(8,128)(2,1)S(1)} %get-tuple-element.64), channel_id=1, source_target_pairs={{0,32},{1,97},{2,34},{3,99},{4,36},{5,101},{6,38},{7,103},{8,40},{... | collective-permute-start | bytes 1572872 | tf_op jit(solution)/shard_map/ppermute | solution.py:35
  204.1 11.3 %collective-permute-start.19 = (bf16[128,2176]{1,0:T(8,128)(2,1)S(1)}, bf16[128,2176]{1,0:T(8,128)(2,1)S(1)}, u32[]{:S(2)}, u32[]{:S(2)}) collective-permute-start(bf16[128,2176]{1,0:T(8,128)(2,1)S(1)} %get-tuple-element.67), channel_id=1, source_target_pairs={{0,8},{1,25},{2,10},{3,27},{4,12},{5,29},{6,14},{7,31},{8,16},{9,1... | collective-permute-start | bytes 1671176 | tf_op jit(solution)/shard_map/ppermute | solution.py:35
  205.6 16.1 %collective-permute-start.28 = (bf16[128,2176]{1,0:T(8,128)(2,1)S(1)}, bf16[128,2176]{1,0:T(8,128)(2,1)S(1)}, u32[]{:S(2)}, u32[]{:S(2)}) collective-permute-start(bf16[128,2176]{1,0:T(8,128)(2,1)S(1)} %get-tuple-element.66), channel_id=1, source_target_pairs={{0,32},{1,97},{2,34},{3,99},{4,36},{5,101},{6,38},{7,103},{8,40},{... | collective-permute-start | bytes 1671176 | tf_op jit(solution)/shard_map/ppermute | solution.py:35
  215.8 12.5 %collective-permute-start.22 = (bf16[32,4224]{1,0:T(8,128)(2,1)S(1)}, bf16[32,4224]{1,0:T(8,128)(2,1)S(1)}, u32[]{:S(2)}, u32[]{:S(2)}) collective-permute-start(bf16[32,4224]{1,0:T(8,128)(2,1)S(1)} %pad_maximum_fusion.6), channel_id=1, source_target_pairs={{0,32},{1,97},{2,34},{3,99},{4,36},{5,101},{6,38},{7,103},{8,40},{... | collective-permute-start | bytes 811016 | tf_op jit(solution)/shard_map/ppermute | solution.py:35
  218.3 12.7 %collective-permute-start.21 = (bf16[32,4224]{1,0:T(8,128)(2,1)S(1)}, bf16[32,4224]{1,0:T(8,128)(2,1)S(1)}, u32[]{:S(2)}, u32[]{:S(2)}) collective-permute-start(bf16[32,4224]{1,0:T(8,128)(2,1)S(1)} %pad_maximum_fusion.5), channel_id=1, source_target_pairs={{0,64},{1,65},{2,66},{3,67},{4,68},{5,69},{6,70},{7,71},{8,72},{9,... | collective-permute-start | bytes 811016 | tf_op jit(solution)/shard_map/ppermute | solution.py:35
  221.3 9.7 %collective-permute-start.20 = (bf16[32,4224]{1,0:T(8,128)(2,1)S(1)}, bf16[32,4224]{1,0:T(8,128)(2,1)S(1)}, u32[]{:S(2)}, u32[]{:S(2)}) collective-permute-start(bf16[32,4224]{1,0:T(8,128)(2,1)S(1)} %pad_maximum_fusion.4), channel_id=1, source_target_pairs={{0,96},{1,33},{2,98},{3,35},{4,100},{5,37},{6,102},{7,39},{8,104},... | collective-permute-start | bytes 811016 | tf_op jit(solution)/shard_map/ppermute | solution.py:35
  222.1 12.6 %collective-permute-start.31 = (bf16[32,4224]{1,0:T(8,128)(2,1)S(1)}, bf16[32,4224]{1,0:T(8,128)(2,1)S(1)}, u32[]{:S(2)}, u32[]{:S(2)}) collective-permute-start(bf16[32,4224]{1,0:T(8,128)(2,1)S(1)} %pad_maximum_fusion.9), channel_id=1, source_target_pairs={{0,8},{1,25},{2,10},{3,27},{4,12},{5,29},{6,14},{7,31},{8,16},{9,1... | collective-permute-start | bytes 811016 | tf_op jit(solution)/shard_map/ppermute | solution.py:35
  223.1 11.5 %collective-permute-start.30 = (bf16[32,4224]{1,0:T(8,128)(2,1)S(1)}, bf16[32,4224]{1,0:T(8,128)(2,1)S(1)}, u32[]{:S(2)}, u32[]{:S(2)}) collective-permute-start(bf16[32,4224]{1,0:T(8,128)(2,1)S(1)} %pad_maximum_fusion.8), channel_id=1, source_target_pairs={{0,16},{1,17},{2,18},{3,19},{4,20},{5,21},{6,22},{7,23},{8,24},{9,... | collective-permute-start | bytes 811016 | tf_op jit(solution)/shard_map/ppermute | solution.py:35
  239.3 7.4 %collective-permute-start.32 = (bf16[64,1152]{1,0:T(8,128)(2,1)S(1)}, bf16[64,1152]{1,0:T(8,128)(2,1)S(1)}, u32[]{:S(2)}, u32[]{:S(2)}) collective-permute-start(bf16[64,1152]{1,0:T(8,128)(2,1)S(1)} %get-tuple-element.73), channel_id=1, source_target_pairs={{0,2},{1,3},{2,4},{3,5},{4,6},{5,7},{6,0},{7,1},{8,10},{9,11},{10,... | collective-permute-start | bytes 442376 | tf_op jit(solution)/shard_map/ppermute | solution.py:27
  (12 other events, 84.6 us)
Sparse Core Ops, SparseCore 0:
  10.5 94.8 all-gather.2

commit v2 on v1

--- a/solution.py
+++ b/solution.py
@@ -229,7 +229,7 @@
         for _ in range(3):
             exits.append(ring(exits[-1], axis))
         if axis == "y":
-            exits, ids = lax.optimization_barrier((jnp.stack(exits), ids))
+            exits = jnp.stack(exits)
 
     names = jnp.arange(32, dtype=jnp.int32)
     member = ids[:, None] == names[None, :]

time: 258 us -> 253 us (0.981)
    ppermute x24, waiting for transfers between devices: 91.6 us -> 71.2 us  [onward(): return lax.ppermute(value, AXES, pairs(move))]
    optimization_barrier x1 -> x0, blocking collectives: 17.7 us -> none  [on_device(): exits, ids = lax.optimization_barrier((jnp.stack(exits), ids))]
    unnamed x0 -> x1, blocking collectives: none -> 16.6 us
    all_gather x1, waiting for transfers between devices: 0.01 us -> 14.7 us  [on_device(): lax.all_gather(tokens, AXES, axis=0, tiled=False).reshape(16, 8, 64, 1024)]
    ppermute x24, starting transfers between devices: 24.4 us -> 17.4 us  [onward(): return lax.ppermute(value, AXES, pairs(move))]
    ppermute x11, starting transfers between devices: 12.4 us -> 18.3 us  [send(): lax.ppermute(value, AXES, pairs(lambda y, z, x, c: (y + dy, z + dz, x + d...]
    ppermute x11, waiting for transfers between devices: 6.18 us -> 11 us  [send(): lax.ppermute(value, AXES, pairs(lambda y, z, x, c: (y + dy, z + dz, x + d...]
  transfers between devices with their start and end apart: 36 -> 36, of which waited for: 21 -> 20; matrix products, arithmetic and copies ran while one was open for 16% -> 16% of each run, Pallas kernels for 11% -> 11%
where the time goes in v2:
time: 253 us; the launch traced here: 251 us
  waiting for transfers between devices  97.5 us (39%)
  Pallas kernels  39.6 us (16%)
  starting transfers between devices  35.8 us (14%)
  matrix products  21.2 us (8%)
  blocking collectives  16.6 us (7%)
  local copies, waits for them, and re-layouts  15.1 us (6%)
  between operations  14.8 us (6%)
  other arithmetic  10.5 us (4%)
    ppermute x24, waiting for transfers between devices, onward(): return lax.ppermute(value, AXES, pairs(move))  71.2 us
    pallas_call x2, Pallas kernels, gate_up(): pl.pallas_call(gate_up_kernel, grid=(4,), in_specs=specs, out_specs=pl.Bl...  18.6 us
    ppermute x11, starting transfers between devices, send(): lax.ppermute(value, AXES, pairs(lambda y, z, x, c: (y + dy, z + dz, x + d...  18.3 us
    ppermute x24, starting transfers between devices, onward(): return lax.ppermute(value, AXES, pairs(move))  17.4 us
    unnamed x1, blocking collectives  16.6 us
    all_gather x1, waiting for transfers between devices, on_device(): lax.all_gather(tokens, AXES, axis=0, tiled=False).reshape(16, 8, 64, 1024)  14.7 us
    ppermute x11, waiting for transfers between devices, send(): lax.ppermute(value, AXES, pairs(lambda y, z, x, c: (y + dy, z + dz, x + d...  11 us
    pallas_call x1, Pallas kernels, hidden_rows(): pl.pallas_call(hidden_kernel, grid_spec=pltpu.PrefetchScalarGridSpec(num_...  10.9 us
  transfers between devices with their start and end apart: 36, of which 20 were waited for; matrix products, arithmetic and copies ran while one was open for 16% of the time, Pallas kernels for 11%

profile of v2, /device:TPU:0, one launch (start us, length us, event | category | flops | bytes accessed | tf_op | source)
XLA Modules:
  0.0 251.2 jit_solution(4527723287165821617)
XLA Ops:
  9.0 6.1 %collective-permute-done = bf16[2,64,1024]{2,1,0:T(8,128)(2,1)S(1)} collective-permute-done((bf16[2,64,1024]{2,1,0:T(8,128)(2,1)}, bf16[2,64,1024]{2,1,0:T(8,128)(2,1)S(1)}, u32[]{:S(2)}, u32[]{:S(2)}) %collective-permute-start) | collective-permute-done | bytes 262176 | tf_op jit(solution)/shard_map/ppermute | solution.py:35
  15.6 7.1 %collective-permute-done.1 = bf16[2,64,1024]{2,1,0:T(8,128)(2,1)S(1)} collective-permute-done((bf16[2,64,1024]{2,1,0:T(8,128)(2,1)S(1)}, bf16[2,64,1024]{2,1,0:T(8,128)(2,1)S(1)}, u32[]{:S(2)}, u32[]{:S(2)}) %collective-permute-start.1) | collective-permute-done | bytes 262176 | tf_op jit(solution)/shard_map/ppermute | solution.py:35
  22.7 8.0 %collective-permute-done.2 = bf16[2,64,1024]{2,1,0:T(8,128)(2,1)S(1)} collective-permute-done((bf16[2,64,1024]{2,1,0:T(8,128)(2,1)S(1)}, bf16[2,64,1024]{2,1,0:T(8,128)(2,1)S(1)}, u32[]{:S(2)}, u32[]{:S(2)}) %collective-permute-start.2) | collective-permute-done | bytes 262176 | tf_op jit(solution)/shard_map/ppermute | solution.py:35
  37.4 13.3 %collective-permute-done.3 = bf16[4,2,64,1024]{3,2,1,0:T(8,128)(2,1)} collective-permute-done((bf16[4,2,64,1024]{3,2,1,0:T(8,128)(2,1)S(1)}, bf16[4,2,64,1024]{3,2,1,0:T(8,128)(2,1)}, u32[]{:S(2)}, u32[]{:S(2)}) %collective-permute-start.3) | collective-permute-done | bytes 1048608 | tf_op jit(solution)/shard_map/ppermute | solution.py:35
  52.8 2.2 dynamic-slice_dynamic-update-slice_fusion.1
  56.7 16.6 %all-reduce.3 = s32[1024]{0:T(1024)S(1)} all-reduce(s32[1024]{0:T(1024)S(1)} %dynamic-update-slice), channel_id=1, replica_groups=mesh['adapter'=16,'tensor'=8] {'adapter'}, use_global_device_ids=true, to_apply=%add.3 | all-reduce | flops 1024 | bytes 8192
  74.0 2.4 dynamic-slice_dynamic-update-slice_fusion
  76.4 3.1 %collective-permute-start.5 = (bf16[4,2,64,1024]{3,2,1,0:T(8,128)(2,1)}, bf16[4,2,64,1024]{3,2,1,0:T(8,128)(2,1)}, u32[]{:S(2)}, u32[]{:S(2)}) collective-permute-start(bf16[4,2,64,1024]{3,2,1,0:T(8,128)(2,1)} %collective-permute-done.4), channel_id=1, source_target_pairs={{0,8},{1,25},{2,10},{3,27},{4,12},{5,29},{6,14},{7,31},{8,16},{9,1... | collective-permute-start | bytes 3145736 | tf_op jit(solution)/shard_map/ppermute | solution.py:35
  82.2 3.3 %fusion.34.row_ref = s32[1024,1]{1,0:T(8,128)} fusion(s32[1024,1]{1,0:T(8,128)S(1)} %copy.23, s32[1024,1]{1,0:T(8,128)} %copy.19, s32[]{:T(128)S(6)} %select_n.243, s32[]{:T(128)S(6)} %select_n.245), kind=kLoop, calls=%fused_computation.82 | loop fusion | flops 69632 | bytes 12296 | tf_op jit(solution)/shard_map/add | solution.py:267
  85.4 14.7 %all-gather.3.cloned.1.call-done = bf16[8192,1024]{1,0:T(8,128)(2,1)} async-done(((bf16[64,1024]{1,0:T(8,128)(2,1)}), bf16[8192,1024]{1,0:T(8,128)(2,1)}) %all-gather.3.cloned.1.call-update) | async-done | bytes 16777232 | tf_op jit(solution)/shard_map/all_gather | solution.py:223
  100.1 10.2 %low_own.1 = bf16[2,80,128]{2,1,0:T(8,128)(2,1)} custom-call(bf16[16,8,64,1024]{3,2,1,0:T(8,128)(2,1)} %bitcast.344, bf16[2,8192,128]{2,1,0:T(8,128)(2,1)} %e_ref.1, bf16[2,80,1024]{2,1,0:T(8,128)(2,1)} %compare_convert_fusion.s_ref), custom_call_target="tpu_custom_call" | custom-call | flops 4294967296 | bytes 22020096 | tf_op jit(solution)/shard_map/low_own/pallas_call | solution.py:74
  112.3 2.5 collective-permute-start.7
  114.8 2.1 collective-permute-start.6
  116.9 9.3 %gate_up.2.refs_0_ = f32[2,512,512]{2,1,0:T(8,128)} custom-call(bf16[16,8,64,1024]{3,2,1,0:T(8,128)(2,1)} %bitcast.345, bf16[224,8192]{1,0:T(8,128)(2,1)} %bitcast.348, bf16[224,8192]{1,0:T(8,128)(2,1)} %bitcast.350), custom_call_target="tpu_custom_call" | custom-call | flops 4294967296 | bytes 16777216 | tf_op jit(solution)/shard_map/gate_up/pallas_call | solution.py:119
  126.2 3.0 %collective-permute-start.11 = (bf16[4,160,128]{2,1,0:T(8,128)(2,1)S(1)}, bf16[4,160,128]{2,1,0:T(8,128)(2,1)S(1)}, u32[]{:S(2)}, u32[]{:S(2)}) collective-permute-start(bf16[4,160,128]{2,1,0:T(8,128)(2,1)S(1)} %get-tuple-element.68), channel_id=1, source_target_pairs={{0,8},{1,9},{2,10},{3,11},{4,12},{5,13},{6,14},{7,15},{8,16},{9,17... | collective-permute-start | bytes 491528 | tf_op jit(solution)/shard_map/ppermute | solution.py:27
  130.4 2.5 %collective-permute-start.9 = (bf16[4,160,128]{2,1,0:T(8,128)(2,1)S(1)}, bf16[4,160,128]{2,1,0:T(8,128)(2,1)S(1)}, u32[]{:S(2)}, u32[]{:S(2)}) collective-permute-start(bf16[4,160,128]{2,1,0:T(8,128)(2,1)S(1)} %get-tuple-element.68), channel_id=1, source_target_pairs={{0,24},{1,25},{2,26},{3,27},{4,28},{5,29},{6,30},{7,31},{8,0},{9,1... | collective-permute-start | bytes 491528 | tf_op jit(solution)/shard_map/ppermute | solution.py:27
  133.0 9.3 %gate_up.3 = f32[2,512,512]{2,1,0:T(8,128)} custom-call(bf16[16,8,64,1024]{3,2,1,0:T(8,128)(2,1)} %bitcast.346, bf16[224,8192]{1,0:T(8,128)(2,1)} %bitcast.349, bf16[224,8192]{1,0:T(8,128)(2,1)} %bitcast.351, f32[2,512,512]{2,1,0:T(8,128)} %gate_up.2.refs_0_), custom_call_target="tpu_custom_call", output_to_operand_aliasing={{}: (3, {})} | custom-call | flops 4294967296 | bytes 16777216 | tf_op jit(solution)/shard_map/gate_up/pallas_call | solution.py:119
  144.2 10.9 %hidden_rows.1 = (bf16[4,2,4,32,384]{4,3,2,1,0:T(8,128)(2,1)}, bf16[4,2,4,32,384]{4,3,2,1,0:T(8,128)(2,1)}) custom-call(s32[8]{0:T(128)} %pad_add_fusion.place, f32[4,256,512]{2,1,0:T(8,128)} %bitcast.374, s32[1024,1]{1,0:T(8,128)} %copy.24.slot_ref, s32[1024,1]{1,0:T(8,128)} %fusion.34.row_ref, bf16[2560,128]{1,0:T(8,128)(2,1)} %bitcast.411, ...), custom_call_target="tpu_custom_call" | custom-call | flops 2684354560 | bytes 16777216 | tf_op jit(solution)/shard_map/hidden_rows/pallas_call | solution.py:179
  156.1 3.4 %convolution_convert_fusion.1 = bf16[256,4224]{1,0:T(8,128)(2,1)S(1)} fusion(bf16[256,384]{1,0:T(8,128)(2,1)S(1)} %bitcast.409, bf16[384,4224]{1,0:T(8,128)(2,1)} %get-tuple-element.36), kind=kOutput, calls=%fused_computation.1 | convolution fusion | flops 831553536 | bytes 5603328 | tf_op jit(solution)/shard_map/dot_general | solution.py:293
  159.6 5.5 %convolution_convert_fusion = bf16[768,4224]{1,0:T(8,128)(2,1)} fusion(bf16[768,384]{1,0:T(8,128)(2,1)S(1)} %bitcast.412, bf16[384,4224]{1,0:T(8,128)(2,1)S(1)} %copy-done), kind=kOutput, calls=%fused_computation | convolution fusion | flops 2494660608 | bytes 10321920 | tf_op jit(solution)/shard_map/dot_general | solution.py:295
  169.2 6.6 %collective-permute-done.13 = bf16[768,4224]{1,0:T(8,128)(2,1)S(1)} collective-permute-done((bf16[768,4224]{1,0:T(8,128)(2,1)}, bf16[768,4224]{1,0:T(8,128)(2,1)S(1)}, u32[]{:S(2)}, u32[]{:S(2)}) %collective-permute-start.13) | collective-permute-done | bytes 6488096 | tf_op jit(solution)/shard_map/ppermute | solution.py:27
  176.3 7.4 %collective-permute-done.23 = bf16[128,2048]{1,0:T(8,128)(2,1)S(1)} collective-permute-done((bf16[128,2048]{1,0:T(8,128)(2,1)S(1)}, bf16[128,2048]{1,0:T(8,128)(2,1)S(1)}, u32[]{:S(2)}, u32[]{:S(2)}) %collective-permute-start.23) | collective-permute-done | bytes 524320 | tf_op jit(solution)/shard_map/ppermute | solution.py:35
  186.0 8.8 %collective-permute-done.24 = bf16[128,2048]{1,0:T(8,128)(2,1)S(1)} collective-permute-done((bf16[128,2048]{1,0:T(8,128)(2,1)S(1)}, bf16[128,2048]{1,0:T(8,128)(2,1)S(1)}, u32[]{:S(2)}, u32[]{:S(2)}) %collective-permute-start.24) | collective-permute-done | bytes 524320 | tf_op jit(solution)/shard_map/ppermute | solution.py:35
  195.8 5.0 %collective-permute-done.27 = bf16[128,2176]{1,0:T(8,128)(2,1)S(1)} collective-permute-done((bf16[128,2176]{1,0:T(8,128)(2,1)S(1)}, bf16[128,2176]{1,0:T(8,128)(2,1)S(1)}, u32[]{:S(2)}, u32[]{:S(2)}) %collective-permute-start.27) | collective-permute-done | bytes 557088 | tf_op jit(solution)/shard_map/ppermute | solution.py:35
  201.7 5.1 %collective-permute-done.16 = bf16[128,2048]{1,0:T(8,128)(2,1)S(1)} collective-permute-done((bf16[128,2048]{1,0:T(8,128)(2,1)S(1)}, bf16[128,2048]{1,0:T(8,128)(2,1)S(1)}, u32[]{:S(2)}, u32[]{:S(2)}) %collective-permute-start.16) | collective-permute-done | bytes 524320 | tf_op jit(solution)/shard_map/ppermute | solution.py:35
  209.2 3.6 %collective-permute-done.19 = bf16[128,2176]{1,0:T(8,128)(2,1)S(1)} collective-permute-done((bf16[128,2176]{1,0:T(8,128)(2,1)S(1)}, bf16[128,2176]{1,0:T(8,128)(2,1)S(1)}, u32[]{:S(2)}, u32[]{:S(2)}) %collective-permute-start.19) | collective-permute-done | bytes 557088 | tf_op jit(solution)/shard_map/ppermute | solution.py:35
  213.7 4.7 %collective-permute-start.21 = (bf16[32,4224]{1,0:T(8,128)(2,1)S(1)}, bf16[32,4224]{1,0:T(8,128)(2,1)S(1)}, u32[]{:S(2)}, u32[]{:S(2)}) collective-permute-start(bf16[32,4224]{1,0:T(8,128)(2,1)S(1)} %pad_maximum_fusion.5), channel_id=1, source_target_pairs={{0,64},{1,65},{2,66},{3,67},{4,68},{5,69},{6,70},{7,71},{8,72},{9,... | collective-permute-start | bytes 811016 | tf_op jit(solution)/shard_map/ppermute | solution.py:35
  223.7 2.6 %collective-permute-start.29 = (bf16[32,4224]{1,0:T(8,128)(2,1)S(1)}, bf16[32,4224]{1,0:T(8,128)(2,1)S(1)}, u32[]{:S(2)}, u32[]{:S(2)}) collective-permute-start(bf16[32,4224]{1,0:T(8,128)(2,1)S(1)} %pad_maximum_fusion.7), channel_id=1, source_target_pairs={{0,24},{1,9},{2,26},{3,11},{4,28},{5,13},{6,30},{7,15},{8,0},{9,17... | collective-permute-start | bytes 811016 | tf_op jit(solution)/shard_map/ppermute | solution.py:35
  228.5 2.9 %collective-permute-done.30 = bf16[32,4224]{1,0:T(8,128)(2,1)S(1)} collective-permute-done((bf16[32,4224]{1,0:T(8,128)(2,1)S(1)}, bf16[32,4224]{1,0:T(8,128)(2,1)S(1)}, u32[]{:S(2)}, u32[]{:S(2)}) %collective-permute-start.30) | collective-permute-done | bytes 270368 | tf_op jit(solution)/shard_map/ppermute | solution.py:35
  231.8 2.7 %collective-permute-start.34 = (bf16[64,1152]{1,0:T(8,128)(2,1)S(1)}, bf16[64,1152]{1,0:T(8,128)(2,1)S(1)}, u32[]{:S(2)}, u32[]{:S(2)}) collective-permute-start(bf16[64,1152]{1,0:T(8,128)(2,1)S(1)} %get-tuple-element.71), channel_id=1, source_target_pairs={{0,6},{1,7},{2,0},{3,1},{4,2},{5,3},{6,4},{7,5},{8,14},{9,15},{10,... | collective-permute-start | bytes 442376 | tf_op jit(solution)/shard_map/ppermute | solution.py:27
  236.2 2.1 pad_maximum_fusion
  238.7 2.5 collective-permute-done.33
  (144 shorter events, 47.0 us)
Async XLA Ops:
  6.5 93.6 %all-gather.3.cloned.1.call-start = ((), (), s32[]{:S(2)}) async-start(), calls=%async_computation | async-start | bytes 16908288 | tf_op jit(solution)/shard_map/all_gather | solution.py:223
  7.3 7.9 %collective-permute-start = (bf16[2,64,1024]{2,1,0:T(8,128)(2,1)}, bf16[2,64,1024]{2,1,0:T(8,128)(2,1)S(1)}, u32[]{:S(2)}, u32[]{:S(2)}) collective-permute-start(bf16[2,64,1024]{2,1,0:T(8,128)(2,1)} %param.21), channel_id=1, source_target_pairs={{0,32},{1,97},{2,34},{3,99},{4,36},{5,101},{6,38},{7,103},{8,40},{... | collective-permute-start | bytes 786440 | tf_op jit(solution)/shard_map/ppermute | solution.py:35
  15.1 7.6 %collective-permute-start.1 = (bf16[2,64,1024]{2,1,0:T(8,128)(2,1)S(1)}, bf16[2,64,1024]{2,1,0:T(8,128)(2,1)S(1)}, u32[]{:S(2)}, u32[]{:S(2)}) collective-permute-start(bf16[2,64,1024]{2,1,0:T(8,128)(2,1)S(1)} %collective-permute-done), channel_id=1, source_target_pairs={{0,32},{1,97},{2,34},{3,99},{4,36},{5,101},{6,38},{7,103},{8,40},{... | collective-permute-start | bytes 786440 | tf_op jit(solution)/shard_map/ppermute | solution.py:35
  22.7 8.0 %collective-permute-start.2 = (bf16[2,64,1024]{2,1,0:T(8,128)(2,1)S(1)}, bf16[2,64,1024]{2,1,0:T(8,128)(2,1)S(1)}, u32[]{:S(2)}, u32[]{:S(2)}) collective-permute-start(bf16[2,64,1024]{2,1,0:T(8,128)(2,1)S(1)} %collective-permute-done.1), channel_id=1, source_target_pairs={{0,32},{1,97},{2,34},{3,99},{4,36},{5,101},{6,38},{7,103},{8,40},{... | collective-permute-start | bytes 786440 | tf_op jit(solution)/shard_map/ppermute | solution.py:35
  31.8 18.9 %collective-permute-start.3 = (bf16[4,2,64,1024]{3,2,1,0:T(8,128)(2,1)S(1)}, bf16[4,2,64,1024]{3,2,1,0:T(8,128)(2,1)}, u32[]{:S(2)}, u32[]{:S(2)}) collective-permute-start(bf16[4,2,64,1024]{3,2,1,0:T(8,128)(2,1)S(1)} %pad_maximum_fusion.2), channel_id=1, source_target_pairs={{0,8},{1,25},{2,10},{3,27},{4,12},{5,29},{6,14},{7,31},{8,16},{9,1... | collective-permute-start | bytes 3145736 | tf_op jit(solution)/shard_map/ppermute | solution.py:35
  50.7 25.7 %collective-permute-start.4 = (bf16[4,2,64,1024]{3,2,1,0:T(8,128)(2,1)}, bf16[4,2,64,1024]{3,2,1,0:T(8,128)(2,1)}, u32[]{:S(2)}, u32[]{:S(2)}) collective-permute-start(bf16[4,2,64,1024]{3,2,1,0:T(8,128)(2,1)} %collective-permute-done.3), channel_id=1, source_target_pairs={{0,8},{1,25},{2,10},{3,27},{4,12},{5,29},{6,14},{7,31},{8,16},{9,1... | collective-permute-start | bytes 3145736 | tf_op jit(solution)/shard_map/ppermute | solution.py:35
  76.4 33.9 %collective-permute-start.5 = (bf16[4,2,64,1024]{3,2,1,0:T(8,128)(2,1)}, bf16[4,2,64,1024]{3,2,1,0:T(8,128)(2,1)}, u32[]{:S(2)}, u32[]{:S(2)}) collective-permute-start(bf16[4,2,64,1024]{3,2,1,0:T(8,128)(2,1)} %collective-permute-done.4), channel_id=1, source_target_pairs={{0,8},{1,25},{2,10},{3,27},{4,12},{5,29},{6,14},{7,31},{8,16},{9,1... | collective-permute-start | bytes 3145736 | tf_op jit(solution)/shard_map/ppermute | solution.py:35
  110.3 15.8 %collective-permute-start.8 = (bf16[160,128]{1,0:T(8,128)(2,1)}, bf16[160,128]{1,0:T(8,128)(2,1)S(1)}, u32[]{:S(2)}, u32[]{:S(2)}) collective-permute-start(bf16[160,128]{1,0:T(8,128)(2,1)} %bitcast.417), channel_id=1, source_target_pairs={{0,32},{1,33},{2,34},{3,35},{4,36},{5,37},{6,38},{7,39},{8,40},{9,... | collective-permute-start | bytes 122888 | tf_op jit(solution)/shard_map/ppermute | solution.py:27
  112.3 13.8 %collective-permute-start.7 = (bf16[160,128]{1,0:T(8,128)(2,1)}, bf16[160,128]{1,0:T(8,128)(2,1)S(1)}, u32[]{:S(2)}, u32[]{:S(2)}) collective-permute-start(bf16[160,128]{1,0:T(8,128)(2,1)} %bitcast.418), channel_id=1, source_target_pairs={{0,64},{1,65},{2,66},{3,67},{4,68},{5,69},{6,70},{7,71},{8,72},{9,... | collective-permute-start | bytes 122888 | tf_op jit(solution)/shard_map/ppermute | solution.py:27
  114.8 11.4 %collective-permute-start.6 = (bf16[160,128]{1,0:T(8,128)(2,1)}, bf16[160,128]{1,0:T(8,128)(2,1)S(1)}, u32[]{:S(2)}, u32[]{:S(2)}) collective-permute-start(bf16[160,128]{1,0:T(8,128)(2,1)} %bitcast.419), channel_id=1, source_target_pairs={{0,96},{1,97},{2,98},{3,99},{4,100},{5,101},{6,102},{7,103},{8,104... | collective-permute-start | bytes 122888 | tf_op jit(solution)/shard_map/ppermute | solution.py:27
  126.2 17.1 %collective-permute-start.11 = (bf16[4,160,128]{2,1,0:T(8,128)(2,1)S(1)}, bf16[4,160,128]{2,1,0:T(8,128)(2,1)S(1)}, u32[]{:S(2)}, u32[]{:S(2)}) collective-permute-start(bf16[4,160,128]{2,1,0:T(8,128)(2,1)S(1)} %get-tuple-element.68), channel_id=1, source_target_pairs={{0,8},{1,9},{2,10},{3,11},{4,12},{5,13},{6,14},{7,15},{8,16},{9,17... | collective-permute-start | bytes 491528 | tf_op jit(solution)/shard_map/ppermute | solution.py:27
  129.2 14.1 %collective-permute-start.10 = (bf16[4,160,128]{2,1,0:T(8,128)(2,1)S(1)}, bf16[4,160,128]{2,1,0:T(8,128)(2,1)S(1)}, u32[]{:S(2)}, u32[]{:S(2)}) collective-permute-start(bf16[4,160,128]{2,1,0:T(8,128)(2,1)S(1)} %get-tuple-element.68), channel_id=1, source_target_pairs={{0,16},{1,17},{2,18},{3,19},{4,20},{5,21},{6,22},{7,23},{8,24},{9,... | collective-permute-start | bytes 491528 | tf_op jit(solution)/shard_map/ppermute | solution.py:27
  130.4 12.9 %collective-permute-start.9 = (bf16[4,160,128]{2,1,0:T(8,128)(2,1)S(1)}, bf16[4,160,128]{2,1,0:T(8,128)(2,1)S(1)}, u32[]{:S(2)}, u32[]{:S(2)}) collective-permute-start(bf16[4,160,128]{2,1,0:T(8,128)(2,1)S(1)} %get-tuple-element.68), channel_id=1, source_target_pairs={{0,24},{1,25},{2,26},{3,27},{4,28},{5,29},{6,30},{7,31},{8,0},{9,1... | collective-permute-start | bytes 491528 | tf_op jit(solution)/shard_map/ppermute | solution.py:27
  165.1 10.8 %collective-permute-start.13 = (bf16[768,4224]{1,0:T(8,128)(2,1)}, bf16[768,4224]{1,0:T(8,128)(2,1)S(1)}, u32[]{:S(2)}, u32[]{:S(2)}) collective-permute-start(bf16[768,4224]{1,0:T(8,128)(2,1)} %convolution_convert_fusion), channel_id=1, source_target_pairs={{0,1},{1,0},{2,3},{3,2},{4,5},{5,4},{6,7},{7,6},{8,9},{9,8},{10,11... | collective-permute-start | bytes 19464200 | tf_op jit(solution)/shard_map/ppermute | solution.py:27
  167.3 17.5 %collective-permute-start.26 = (bf16[128,2176]{1,0:T(8,128)(2,1)S(1)}, bf16[128,2176]{1,0:T(8,128)(2,1)S(1)}, u32[]{:S(2)}, u32[]{:S(2)}) collective-permute-start(bf16[128,2176]{1,0:T(8,128)(2,1)S(1)} %fusion.2), channel_id=1, source_target_pairs={{0,32},{1,97},{2,34},{3,99},{4,36},{5,101},{6,38},{7,103},{8,40},{... | collective-permute-start | bytes 1671176 | tf_op jit(solution)/shard_map/ppermute | solution.py:35
  167.4 18.0 %collective-permute-start.17 = (bf16[128,2176]{1,0:T(8,128)(2,1)S(1)}, bf16[128,2176]{1,0:T(8,128)(2,1)S(1)}, u32[]{:S(2)}, u32[]{:S(2)}) collective-permute-start(bf16[128,2176]{1,0:T(8,128)(2,1)S(1)} %fusion.1), channel_id=1, source_target_pairs={{0,8},{1,25},{2,10},{3,27},{4,12},{5,29},{6,14},{7,31},{8,16},{9,1... | collective-permute-start | bytes 1671176 | tf_op jit(solution)/shard_map/ppermute | solution.py:35
  167.5 16.3 %collective-permute-start.23 = (bf16[128,2048]{1,0:T(8,128)(2,1)S(1)}, bf16[128,2048]{1,0:T(8,128)(2,1)S(1)}, u32[]{:S(2)}, u32[]{:S(2)}) collective-permute-start(bf16[128,2048]{1,0:T(8,128)(2,1)S(1)} %fusion.4), channel_id=1, source_target_pairs={{0,32},{1,97},{2,34},{3,99},{4,36},{5,101},{6,38},{7,103},{8,40},{... | collective-permute-start | bytes 1572872 | tf_op jit(solution)/shard_map/ppermute | solution.py:35
  167.6 16.8 %collective-permute-start.14 = (bf16[128,2048]{1,0:T(8,128)(2,1)S(1)}, bf16[128,2048]{1,0:T(8,128)(2,1)S(1)}, u32[]{:S(2)}, u32[]{:S(2)}) collective-permute-start(bf16[128,2048]{1,0:T(8,128)(2,1)S(1)} %fusion.3), channel_id=1, source_target_pairs={{0,8},{1,25},{2,10},{3,27},{4,12},{5,29},{6,14},{7,31},{8,16},{9,1... | collective-permute-start | bytes 1572872 | tf_op jit(solution)/shard_map/ppermute | solution.py:35
  184.1 10.7 %collective-permute-start.24 = (bf16[128,2048]{1,0:T(8,128)(2,1)S(1)}, bf16[128,2048]{1,0:T(8,128)(2,1)S(1)}, u32[]{:S(2)}, u32[]{:S(2)}) collective-permute-start(bf16[128,2048]{1,0:T(8,128)(2,1)S(1)} %fusion.18), channel_id=1, source_target_pairs={{0,32},{1,97},{2,34},{3,99},{4,36},{5,101},{6,38},{7,103},{8,40},{... | collective-permute-start | bytes 1572872 | tf_op jit(solution)/shard_map/ppermute | solution.py:35
  184.8 10.5 %collective-permute-start.15 = (bf16[128,2048]{1,0:T(8,128)(2,1)S(1)}, bf16[128,2048]{1,0:T(8,128)(2,1)S(1)}, u32[]{:S(2)}, u32[]{:S(2)}) collective-permute-start(bf16[128,2048]{1,0:T(8,128)(2,1)S(1)} %fusion.22), channel_id=1, source_target_pairs={{0,8},{1,25},{2,10},{3,27},{4,12},{5,29},{6,14},{7,31},{8,16},{9,1... | collective-permute-start | bytes 1572872 | tf_op jit(solution)/shard_map/ppermute | solution.py:35
  185.3 15.4 %collective-permute-start.27 = (bf16[128,2176]{1,0:T(8,128)(2,1)S(1)}, bf16[128,2176]{1,0:T(8,128)(2,1)S(1)}, u32[]{:S(2)}, u32[]{:S(2)}) collective-permute-start(bf16[128,2176]{1,0:T(8,128)(2,1)S(1)} %fusion.9), channel_id=1, source_target_pairs={{0,32},{1,97},{2,34},{3,99},{4,36},{5,101},{6,38},{7,103},{8,40},{... | collective-permute-start | bytes 1671176 | tf_op jit(solution)/shard_map/ppermute | solution.py:35
  185.9 15.3 %collective-permute-start.18 = (bf16[128,2176]{1,0:T(8,128)(2,1)S(1)}, bf16[128,2176]{1,0:T(8,128)(2,1)S(1)}, u32[]{:S(2)}, u32[]{:S(2)}) collective-permute-start(bf16[128,2176]{1,0:T(8,128)(2,1)S(1)} %fusion.13), channel_id=1, source_target_pairs={{0,8},{1,25},{2,10},{3,27},{4,12},{5,29},{6,14},{7,31},{8,16},{9,1... | collective-permute-start | bytes 1671176 | tf_op jit(solution)/shard_map/ppermute | solution.py:35
  195.6 11.2 %collective-permute-start.16 = (bf16[128,2048]{1,0:T(8,128)(2,1)S(1)}, bf16[128,2048]{1,0:T(8,128)(2,1)S(1)}, u32[]{:S(2)}, u32[]{:S(2)}) collective-permute-start(bf16[128,2048]{1,0:T(8,128)(2,1)S(1)} %get-tuple-element.61), channel_id=1, source_target_pairs={{0,8},{1,25},{2,10},{3,27},{4,12},{5,29},{6,14},{7,31},{8,16},{9,1... | collective-permute-start | bytes 1572872 | tf_op jit(solution)/shard_map/ppermute | solution.py:35
  195.7 12.0 %collective-permute-start.25 = (bf16[128,2048]{1,0:T(8,128)(2,1)S(1)}, bf16[128,2048]{1,0:T(8,128)(2,1)S(1)}, u32[]{:S(2)}, u32[]{:S(2)}) collective-permute-start(bf16[128,2048]{1,0:T(8,128)(2,1)S(1)} %get-tuple-element.60), channel_id=1, source_target_pairs={{0,32},{1,97},{2,34},{3,99},{4,36},{5,101},{6,38},{7,103},{8,40},{... | collective-permute-start | bytes 1572872 | tf_op jit(solution)/shard_map/ppermute | solution.py:35
  201.5 11.3 %collective-permute-start.19 = (bf16[128,2176]{1,0:T(8,128)(2,1)S(1)}, bf16[128,2176]{1,0:T(8,128)(2,1)S(1)}, u32[]{:S(2)}, u32[]{:S(2)}) collective-permute-start(bf16[128,2176]{1,0:T(8,128)(2,1)S(1)} %get-tuple-element.63), channel_id=1, source_target_pairs={{0,8},{1,25},{2,10},{3,27},{4,12},{5,29},{6,14},{7,31},{8,16},{9,1... | collective-permute-start | bytes 1671176 | tf_op jit(solution)/shard_map/ppermute | solution.py:35
  201.6 17.4 %collective-permute-start.28 = (bf16[128,2176]{1,0:T(8,128)(2,1)S(1)}, bf16[128,2176]{1,0:T(8,128)(2,1)S(1)}, u32[]{:S(2)}, u32[]{:S(2)}) collective-permute-start(bf16[128,2176]{1,0:T(8,128)(2,1)S(1)} %get-tuple-element.62), channel_id=1, source_target_pairs={{0,32},{1,97},{2,34},{3,99},{4,36},{5,101},{6,38},{7,103},{8,40},{... | collective-permute-start | bytes 1671176 | tf_op jit(solution)/shard_map/ppermute | solution.py:35
  213.2 10.5 %collective-permute-start.22 = (bf16[32,4224]{1,0:T(8,128)(2,1)S(1)}, bf16[32,4224]{1,0:T(8,128)(2,1)S(1)}, u32[]{:S(2)}, u32[]{:S(2)}) collective-permute-start(bf16[32,4224]{1,0:T(8,128)(2,1)S(1)} %pad_maximum_fusion.6), channel_id=1, source_target_pairs={{0,32},{1,97},{2,34},{3,99},{4,36},{5,101},{6,38},{7,103},{8,40},{... | collective-permute-start | bytes 811016 | tf_op jit(solution)/shard_map/ppermute | solution.py:35
  213.7 12.9 %collective-permute-start.21 = (bf16[32,4224]{1,0:T(8,128)(2,1)S(1)}, bf16[32,4224]{1,0:T(8,128)(2,1)S(1)}, u32[]{:S(2)}, u32[]{:S(2)}) collective-permute-start(bf16[32,4224]{1,0:T(8,128)(2,1)S(1)} %pad_maximum_fusion.5), channel_id=1, source_target_pairs={{0,64},{1,65},{2,66},{3,67},{4,68},{5,69},{6,70},{7,71},{8,72},{9,... | collective-permute-start | bytes 811016 | tf_op jit(solution)/shard_map/ppermute | solution.py:35
  218.9 7.7 %collective-permute-start.20 = (bf16[32,4224]{1,0:T(8,128)(2,1)S(1)}, bf16[32,4224]{1,0:T(8,128)(2,1)S(1)}, u32[]{:S(2)}, u32[]{:S(2)}) collective-permute-start(bf16[32,4224]{1,0:T(8,128)(2,1)S(1)} %pad_maximum_fusion.4), channel_id=1, source_target_pairs={{0,96},{1,33},{2,98},{3,35},{4,100},{5,37},{6,102},{7,39},{8,104},... | collective-permute-start | bytes 811016 | tf_op jit(solution)/shard_map/ppermute | solution.py:35
  219.4 9.1 %collective-permute-start.31 = (bf16[32,4224]{1,0:T(8,128)(2,1)S(1)}, bf16[32,4224]{1,0:T(8,128)(2,1)S(1)}, u32[]{:S(2)}, u32[]{:S(2)}) collective-permute-start(bf16[32,4224]{1,0:T(8,128)(2,1)S(1)} %pad_maximum_fusion.9), channel_id=1, source_target_pairs={{0,8},{1,25},{2,10},{3,27},{4,12},{5,29},{6,14},{7,31},{8,16},{9,1... | collective-permute-start | bytes 811016 | tf_op jit(solution)/shard_map/ppermute | solution.py:35
  220.0 11.5 %collective-permute-start.30 = (bf16[32,4224]{1,0:T(8,128)(2,1)S(1)}, bf16[32,4224]{1,0:T(8,128)(2,1)S(1)}, u32[]{:S(2)}, u32[]{:S(2)}) collective-permute-start(bf16[32,4224]{1,0:T(8,128)(2,1)S(1)} %pad_maximum_fusion.8), channel_id=1, source_target_pairs={{0,16},{1,17},{2,18},{3,19},{4,20},{5,21},{6,22},{7,23},{8,24},{9,... | collective-permute-start | bytes 811016 | tf_op jit(solution)/shard_map/ppermute | solution.py:35
  223.7 7.8 %collective-permute-start.29 = (bf16[32,4224]{1,0:T(8,128)(2,1)S(1)}, bf16[32,4224]{1,0:T(8,128)(2,1)S(1)}, u32[]{:S(2)}, u32[]{:S(2)}) collective-permute-start(bf16[32,4224]{1,0:T(8,128)(2,1)S(1)} %pad_maximum_fusion.7), channel_id=1, source_target_pairs={{0,24},{1,9},{2,26},{3,11},{4,28},{5,13},{6,30},{7,15},{8,0},{9,17... | collective-permute-start | bytes 811016 | tf_op jit(solution)/shard_map/ppermute | solution.py:35
  (13 other events, 85.9 us)
Sparse Core Ops, SparseCore 0:
  10.5 89.5 all-gather.2

commit v3 on v2

--- a/solution.py
+++ b/solution.py
@@ -263,11 +263,10 @@
     theirs = columns(turns, 1 - c, 384, True)
     mine = (columns((1, 2), c, 256, False), columns((3, 0), c, 384, True))
 
-    every, select, slot, row, theirs, mine = lax.optimization_barrier(
-        (every, select, slot, (relative * 160 + row)[:, None], theirs, mine)
+    every, exits, select, slot, row, theirs, mine = lax.optimization_barrier(
+        (every, exits, select, slot, (relative * 160 + row)[:, None], theirs, mine)
     )
     low_own = low_own_rows(every, adapter_entry_maps, select).reshape(160, 128)
-    low_own, exits = lax.optimization_barrier((low_own, exits))
     exits = jnp.stack(exits).reshape(2048, 1024)
     low = jnp.stack([low_own] + [send(low_own, dy=-d) for d in (1, 2, 3)])
     low = jnp.stack([low] + [send(low, dz=-d) for d in (1, 2, 3)]).reshape(2560, 128)

time: 253 us -> 249 us (0.984)
  waiting for transfers between devices: 97.5 us -> 87.7 us
  starting transfers between devices: 35.8 us -> 42.6 us
    all_gather x1, waiting for transfers between devices: 14.7 us -> 0.01 us  [on_device(): lax.all_gather(tokens, AXES, axis=0, tiled=False).reshape(16, 8, 64, 1024)]
    ppermute x24, starting transfers between devices: 17.4 us -> 30 us  [onward(): return lax.ppermute(value, AXES, pairs(move))]
    ppermute x24, waiting for transfers between devices: 71.2 us -> 80.3 us  [onward(): return lax.ppermute(value, AXES, pairs(move))]
    ppermute x11, starting transfers between devices: 18.3 us -> 12.6 us  [send(): lax.ppermute(value, AXES, pairs(lambda y, z, x, c: (y + dy, z + dz, x + d...]
    ppermute x11, waiting for transfers between devices: 11 us -> 6.68 us  [send(): lax.ppermute(value, AXES, pairs(lambda y, z, x, c: (y + dy, z + dz, x + d...]
  transfers between devices with their start and end apart: 36 -> 36, of which waited for: 20 -> 17; matrix products, arithmetic and copies ran while one was open for 16% -> 15% of each run, Pallas kernels for 11% -> 8%
where the time goes in v3:
time: 249 us; the launch traced here: 247 us
  waiting for transfers between devices  87.7 us (35%)
  starting transfers between devices  42.6 us (17%)
  Pallas kernels  39.6 us (16%)
  matrix products  19.6 us (8%)
  blocking collectives  18.8 us (8%)
  local copies, waits for them, and re-layouts  15.2 us (6%)
  between operations  14.7 us (6%)
  other arithmetic  8.44 us (3%)
    ppermute x24, waiting for transfers between devices, onward(): return lax.ppermute(value, AXES, pairs(move))  80.3 us
    ppermute x24, starting transfers between devices, onward(): return lax.ppermute(value, AXES, pairs(move))  30 us
    unnamed x1, blocking collectives  18.8 us
    pallas_call x2, Pallas kernels, gate_up(): pl.pallas_call(gate_up_kernel, grid=(4,), in_specs=specs, out_specs=pl.Bl...  18.5 us
    ppermute x11, starting transfers between devices, send(): lax.ppermute(value, AXES, pairs(lambda y, z, x, c: (y + dy, z + dz, x + d...  12.6 us
    pallas_call x1, Pallas kernels, hidden_rows(): pl.pallas_call(hidden_kernel, grid_spec=pltpu.PrefetchScalarGridSpec(num_...  10.9 us
    dot_general x28, matrix products, own_part(): part = jnp.dot(h, mine[ch], preferred_element_type=F32)  10.4 us
    pallas_call x1, Pallas kernels, low_own_rows(): pl.pallas_call(low_kernel, grid=(4,), in_specs=[pl.BlockSpec((16, 2, 64,...  10.2 us
  transfers between devices with their start and end apart: 36, of which 17 were waited for; matrix products, arithmetic and copies ran while one was open for 15% of the time, Pallas kernels for 8%

profile of v3, /device:TPU:0, one launch (start us, length us, event | category | flops | bytes accessed | tf_op | source)
XLA Modules:
  0.0 246.6 jit_solution(14306268648381317339)
XLA Ops:
  9.0 6.1 %collective-permute-done = bf16[2,64,1024]{2,1,0:T(8,128)(2,1)S(1)} collective-permute-done((bf16[2,64,1024]{2,1,0:T(8,128)(2,1)}, bf16[2,64,1024]{2,1,0:T(8,128)(2,1)S(1)}, u32[]{:S(2)}, u32[]{:S(2)}) %collective-permute-start) | collective-permute-done | bytes 262176 | tf_op jit(solution)/shard_map/ppermute | solution.py:35
  15.6 7.1 %collective-permute-done.1 = bf16[2,64,1024]{2,1,0:T(8,128)(2,1)S(1)} collective-permute-done((bf16[2,64,1024]{2,1,0:T(8,128)(2,1)S(1)}, bf16[2,64,1024]{2,1,0:T(8,128)(2,1)S(1)}, u32[]{:S(2)}, u32[]{:S(2)}) %collective-permute-start.1) | collective-permute-done | bytes 262176 | tf_op jit(solution)/shard_map/ppermute | solution.py:35
  22.7 8.0 %collective-permute-done.2 = bf16[2,64,1024]{2,1,0:T(8,128)(2,1)S(1)} collective-permute-done((bf16[2,64,1024]{2,1,0:T(8,128)(2,1)S(1)}, bf16[2,64,1024]{2,1,0:T(8,128)(2,1)S(1)}, u32[]{:S(2)}, u32[]{:S(2)}) %collective-permute-start.2) | collective-permute-done | bytes 262176 | tf_op jit(solution)/shard_map/ppermute | solution.py:35
  33.6 17.0 %collective-permute-done.3 = bf16[4,2,64,1024]{3,2,1,0:T(8,128)(2,1)S(1)} collective-permute-done((bf16[4,2,64,1024]{3,2,1,0:T(8,128)(2,1)S(1)}, bf16[4,2,64,1024]{3,2,1,0:T(8,128)(2,1)S(1)}, u32[]{:S(2)}, u32[]{:S(2)}) %collective-permute-start.3) | collective-permute-done | bytes 1048608 | tf_op jit(solution)/shard_map/ppermute | solution.py:35
  50.6 1.9 pad.9
  54.3 18.8 %all-reduce.3 = s32[1024]{0:T(1024)S(1)} all-reduce(s32[1024]{0:T(1024)S(1)} %dynamic-update-slice), channel_id=1, replica_groups=mesh['adapter'=16,'tensor'=8] {'adapter'}, use_global_device_ids=true, to_apply=%add.3 | all-reduce | flops 1024 | bytes 8192
  77.4 2.4 dynamic-slice_dynamic-update-slice_fusion.1
  79.8 3.0 %collective-permute-start.5 = (bf16[4,2,64,1024]{3,2,1,0:T(8,128)(2,1)}, bf16[4,2,64,1024]{3,2,1,0:T(8,128)(2,1)}, u32[]{:S(2)}, u32[]{:S(2)}) collective-permute-start(bf16[4,2,64,1024]{3,2,1,0:T(8,128)(2,1)} %collective-permute-done.4), channel_id=1, source_target_pairs={{0,8},{1,25},{2,10},{3,27},{4,12},{5,29},{6,14},{7,31},{8,16},{9,1... | collective-permute-start | bytes 3145736 | tf_op jit(solution)/shard_map/ppermute | solution.py:35
  84.8 2.3 dynamic-slice_dynamic-update-slice_fusion
  88.0 2.2 fusion.62.row_ref
  90.2 13.2 %collective-permute-done.5 = bf16[4,2,64,1024]{3,2,1,0:T(8,128)(2,1)} collective-permute-done((bf16[4,2,64,1024]{3,2,1,0:T(8,128)(2,1)}, bf16[4,2,64,1024]{3,2,1,0:T(8,128)(2,1)}, u32[]{:S(2)}, u32[]{:S(2)}) %collective-permute-start.5) | collective-permute-done | bytes 1048608 | tf_op jit(solution)/shard_map/ppermute | solution.py:35
  103.4 10.2 %low_own.1 = bf16[2,80,128]{2,1,0:T(8,128)(2,1)} custom-call(bf16[16,8,64,1024]{3,2,1,0:T(8,128)(2,1)} %bitcast.304, bf16[2,8192,128]{2,1,0:T(8,128)(2,1)} %e_ref.1, bf16[2,80,1024]{2,1,0:T(8,128)(2,1)} %compare_convert_fusion.s_ref), custom_call_target="tpu_custom_call" | custom-call | flops 4294967296 | bytes 22020096 | tf_op jit(solution)/shard_map/low_own/pallas_call | solution.py:74
  113.6 2.7 %collective-permute-start.6 = (bf16[160,128]{1,0:T(8,128)(2,1)}, bf16[160,128]{1,0:T(8,128)(2,1)S(1)}, u32[]{:S(2)}, u32[]{:S(2)}) collective-permute-start(bf16[160,128]{1,0:T(8,128)(2,1)} %bitcast.380), channel_id=1, source_target_pairs={{0,96},{1,97},{2,98},{3,99},{4,100},{5,101},{6,102},{7,103},{8,104... | collective-permute-start | bytes 122888 | tf_op jit(solution)/shard_map/ppermute | solution.py:27
  118.0 9.3 %gate_up.2.refs_0_ = f32[2,512,512]{2,1,0:T(8,128)} custom-call(bf16[16,8,64,1024]{3,2,1,0:T(8,128)(2,1)} %bitcast.305, bf16[224,8192]{1,0:T(8,128)(2,1)} %bitcast.308, bf16[224,8192]{1,0:T(8,128)(2,1)} %bitcast.310), custom_call_target="tpu_custom_call" | custom-call | flops 4294967296 | bytes 16777216 | tf_op jit(solution)/shard_map/gate_up/pallas_call | solution.py:119
  129.5 9.3 %gate_up.3 = f32[2,512,512]{2,1,0:T(8,128)} custom-call(bf16[16,8,64,1024]{3,2,1,0:T(8,128)(2,1)} %bitcast.306, bf16[224,8192]{1,0:T(8,128)(2,1)} %bitcast.309, bf16[224,8192]{1,0:T(8,128)(2,1)} %bitcast.311, f32[2,512,512]{2,1,0:T(8,128)} %gate_up.2.refs_0_), custom_call_target="tpu_custom_call", output_to_operand_aliasing={{}: (3, {})} | custom-call | flops 4294967296 | bytes 16777216 | tf_op jit(solution)/shard_map/gate_up/pallas_call | solution.py:119
  140.8 10.9 %hidden_rows.1 = (bf16[4,2,4,32,384]{4,3,2,1,0:T(8,128)(2,1)}, bf16[4,2,4,32,384]{4,3,2,1,0:T(8,128)(2,1)}) custom-call(s32[8]{0:T(128)} %pad_add_fusion.place, f32[4,256,512]{2,1,0:T(8,128)} %bitcast.336, s32[1024,1]{1,0:T(8,128)} %copy.24.slot_ref, s32[1024,1]{1,0:T(8,128)} %fusion.62.row_ref, bf16[2560,128]{1,0:T(8,128)(2,1)} %bitcast.374, ...), custom_call_target="tpu_custom_call" | custom-call | flops 2684354560 | bytes 16777216 | tf_op jit(solution)/shard_map/hidden_rows/pallas_call | solution.py:179
  152.6 3.4 %convolution_convert_fusion.1 = bf16[256,4224]{1,0:T(8,128)(2,1)S(1)} fusion(bf16[256,384]{1,0:T(8,128)(2,1)S(1)} %bitcast.372, bf16[384,4224]{1,0:T(8,128)(2,1)} %get-tuple-element.34), kind=kOutput, calls=%fused_computation.1 | convolution fusion | flops 831553536 | bytes 5603328 | tf_op jit(solution)/shard_map/dot_general | solution.py:292
  156.2 3.8 %convolution_convert_fusion = bf16[768,4224]{1,0:T(8,128)(2,1)S(1)} fusion(bf16[768,384]{1,0:T(8,128)(2,1)S(1)} %bitcast.375, bf16[384,4224]{1,0:T(8,128)(2,1)S(1)} %copy-done), kind=kOutput, calls=%fused_computation | convolution fusion | flops 2494660608 | bytes 10321920 | tf_op jit(solution)/shard_map/dot_general | solution.py:294
  164.3 2.1 collective-permute-start.14
  168.3 2.5 %collective-permute-done.13 = bf16[768,4224]{1,0:T(8,128)(2,1)S(1)} collective-permute-done((bf16[768,4224]{1,0:T(8,128)(2,1)S(1)}, bf16[768,4224]{1,0:T(8,128)(2,1)S(1)}, u32[]{:S(2)}, u32[]{:S(2)}) %collective-permute-start.13) | collective-permute-done | bytes 6488096 | tf_op jit(solution)/shard_map/ppermute | solution.py:27
  173.8 5.0 %collective-permute-done.26 = bf16[128,2176]{1,0:T(8,128)(2,1)S(1)} collective-permute-done((bf16[128,2176]{1,0:T(8,128)(2,1)S(1)}, bf16[128,2176]{1,0:T(8,128)(2,1)S(1)}, u32[]{:S(2)}, u32[]{:S(2)}) %collective-permute-start.26) | collective-permute-done | bytes 557088 | tf_op jit(solution)/shard_map/ppermute | solution.py:35
  180.2 2.4 collective-permute-start.15
  183.1 1.9 collective-permute-start.18
  185.5 5.4 %collective-permute-done.15 = bf16[128,2048]{1,0:T(8,128)(2,1)S(1)} collective-permute-done((bf16[128,2048]{1,0:T(8,128)(2,1)S(1)}, bf16[128,2048]{1,0:T(8,128)(2,1)S(1)}, u32[]{:S(2)}, u32[]{:S(2)}) %collective-permute-start.15) | collective-permute-done | bytes 524320 | tf_op jit(solution)/shard_map/ppermute | solution.py:35
  192.8 4.1 %collective-permute-done.18 = bf16[128,2176]{1,0:T(8,128)(2,1)S(1)} collective-permute-done((bf16[128,2176]{1,0:T(8,128)(2,1)S(1)}, bf16[128,2176]{1,0:T(8,128)(2,1)S(1)}, u32[]{:S(2)}, u32[]{:S(2)}) %collective-permute-start.18) | collective-permute-done | bytes 557088 | tf_op jit(solution)/shard_map/ppermute | solution.py:35
  199.2 3.2 %collective-permute-done.16 = bf16[128,2048]{1,0:T(8,128)(2,1)S(1)} collective-permute-done((bf16[128,2048]{1,0:T(8,128)(2,1)S(1)}, bf16[128,2048]{1,0:T(8,128)(2,1)S(1)}, u32[]{:S(2)}, u32[]{:S(2)}) %collective-permute-start.16) | collective-permute-done | bytes 524320 | tf_op jit(solution)/shard_map/ppermute | solution.py:35
  204.4 1.9 collective-permute-start.29
  210.2 4.0 %collective-permute-start.20 = (bf16[32,4224]{1,0:T(8,128)(2,1)S(1)}, bf16[32,4224]{1,0:T(8,128)(2,1)S(1)}, u32[]{:S(2)}, u32[]{:S(2)}) collective-permute-start(bf16[32,4224]{1,0:T(8,128)(2,1)S(1)} %pad_maximum_fusion.4), channel_id=1, source_target_pairs={{0,96},{1,33},{2,98},{3,35},{4,100},{5,37},{6,102},{7,39},{8,104},... | collective-permute-start | bytes 811016 | tf_op jit(solution)/shard_map/ppermute | solution.py:35
  217.9 3.0 %collective-permute-done.31 = bf16[32,4224]{1,0:T(8,128)(2,1)S(1)} collective-permute-done((bf16[32,4224]{1,0:T(8,128)(2,1)S(1)}, bf16[32,4224]{1,0:T(8,128)(2,1)S(1)}, u32[]{:S(2)}, u32[]{:S(2)}) %collective-permute-start.31) | collective-permute-done | bytes 270368 | tf_op jit(solution)/shard_map/ppermute | solution.py:35
  221.0 5.4 %collective-permute-done.20 = bf16[32,4224]{1,0:T(8,128)(2,1)S(1)} collective-permute-done((bf16[32,4224]{1,0:T(8,128)(2,1)S(1)}, bf16[32,4224]{1,0:T(8,128)(2,1)S(1)}, u32[]{:S(2)}, u32[]{:S(2)}) %collective-permute-start.20) | collective-permute-done | bytes 270368 | tf_op jit(solution)/shard_map/ppermute | solution.py:35
  228.2 2.7 %collective-permute-start.33 = (bf16[64,1152]{1,0:T(8,128)(2,1)S(1)}, bf16[64,1152]{1,0:T(8,128)(2,1)S(1)}, u32[]{:S(2)}, u32[]{:S(2)}) collective-permute-start(bf16[64,1152]{1,0:T(8,128)(2,1)S(1)} %get-tuple-element.64), channel_id=1, source_target_pairs={{0,4},{1,5},{2,6},{3,7},{4,0},{5,1},{6,2},{7,3},{8,12},{9,13},{10,... | collective-permute-start | bytes 442376 | tf_op jit(solution)/shard_map/ppermute | solution.py:27
  234.2 3.8 %collective-permute-done.33 = bf16[64,1152]{1,0:T(8,128)(2,1)S(1)} collective-permute-done((bf16[64,1152]{1,0:T(8,128)(2,1)S(1)}, bf16[64,1152]{1,0:T(8,128)(2,1)S(1)}, u32[]{:S(2)}, u32[]{:S(2)}) %collective-permute-start.33) | collective-permute-done | bytes 147488 | tf_op jit(solution)/shard_map/ppermute | solution.py:27
  (148 shorter events, 52.9 us)
Async XLA Ops:
  6.5 96.9 %all-gather.3.cloned.1.call-start = ((), (), s32[]{:S(2)}) async-start(), calls=%async_computation | async-start | bytes 16908288 | tf_op jit(solution)/shard_map/all_gather | solution.py:223
  7.3 7.9 %collective-permute-start = (bf16[2,64,1024]{2,1,0:T(8,128)(2,1)}, bf16[2,64,1024]{2,1,0:T(8,128)(2,1)S(1)}, u32[]{:S(2)}, u32[]{:S(2)}) collective-permute-start(bf16[2,64,1024]{2,1,0:T(8,128)(2,1)} %param.21), channel_id=1, source_target_pairs={{0,32},{1,97},{2,34},{3,99},{4,36},{5,101},{6,38},{7,103},{8,40},{... | collective-permute-start | bytes 786440 | tf_op jit(solution)/shard_map/ppermute | solution.py:35
  22.7 8.0 %collective-permute-start.2 = (bf16[2,64,1024]{2,1,0:T(8,128)(2,1)S(1)}, bf16[2,64,1024]{2,1,0:T(8,128)(2,1)S(1)}, u32[]{:S(2)}, u32[]{:S(2)}) collective-permute-start(bf16[2,64,1024]{2,1,0:T(8,128)(2,1)S(1)} %collective-permute-done.1), channel_id=1, source_target_pairs={{0,32},{1,97},{2,34},{3,99},{4,36},{5,101},{6,38},{7,103},{8,40},{... | collective-permute-start | bytes 786440 | tf_op jit(solution)/shard_map/ppermute | solution.py:35
  31.8 18.8 %collective-permute-start.3 = (bf16[4,2,64,1024]{3,2,1,0:T(8,128)(2,1)S(1)}, bf16[4,2,64,1024]{3,2,1,0:T(8,128)(2,1)S(1)}, u32[]{:S(2)}, u32[]{:S(2)}) collective-permute-start(bf16[4,2,64,1024]{3,2,1,0:T(8,128)(2,1)S(1)} %pad_maximum_fusion.2), channel_id=1, source_target_pairs={{0,8},{1,25},{2,10},{3,27},{4,12},{5,29},{6,14},{7,31},{8,16},{9,1... | collective-permute-start | bytes 3145736 | tf_op jit(solution)/shard_map/ppermute | solution.py:35
  50.6 29.2 %collective-permute-start.4 = (bf16[4,2,64,1024]{3,2,1,0:T(8,128)(2,1)S(1)}, bf16[4,2,64,1024]{3,2,1,0:T(8,128)(2,1)}, u32[]{:S(2)}, u32[]{:S(2)}) collective-permute-start(bf16[4,2,64,1024]{3,2,1,0:T(8,128)(2,1)S(1)} %collective-permute-done.3), channel_id=1, source_target_pairs={{0,8},{1,25},{2,10},{3,27},{4,12},{5,29},{6,14},{7,31},{8,16},{9,1... | collective-permute-start | bytes 3145736 | tf_op jit(solution)/shard_map/ppermute | solution.py:35
  79.8 23.6 %collective-permute-start.5 = (bf16[4,2,64,1024]{3,2,1,0:T(8,128)(2,1)}, bf16[4,2,64,1024]{3,2,1,0:T(8,128)(2,1)}, u32[]{:S(2)}, u32[]{:S(2)}) collective-permute-start(bf16[4,2,64,1024]{3,2,1,0:T(8,128)(2,1)} %collective-permute-done.4), channel_id=1, source_target_pairs={{0,8},{1,25},{2,10},{3,27},{4,12},{5,29},{6,14},{7,31},{8,16},{9,1... | collective-permute-start | bytes 3145736 | tf_op jit(solution)/shard_map/ppermute | solution.py:35
  113.6 13.7 %collective-permute-start.6 = (bf16[160,128]{1,0:T(8,128)(2,1)}, bf16[160,128]{1,0:T(8,128)(2,1)S(1)}, u32[]{:S(2)}, u32[]{:S(2)}) collective-permute-start(bf16[160,128]{1,0:T(8,128)(2,1)} %bitcast.380), channel_id=1, source_target_pairs={{0,96},{1,97},{2,98},{3,99},{4,100},{5,101},{6,102},{7,103},{8,104... | collective-permute-start | bytes 122888 | tf_op jit(solution)/shard_map/ppermute | solution.py:27
  116.3 11.0 %collective-permute-start.7 = (bf16[160,128]{1,0:T(8,128)(2,1)}, bf16[160,128]{1,0:T(8,128)(2,1)S(1)}, u32[]{:S(2)}, u32[]{:S(2)}) collective-permute-start(bf16[160,128]{1,0:T(8,128)(2,1)} %bitcast.381), channel_id=1, source_target_pairs={{0,64},{1,65},{2,66},{3,67},{4,68},{5,69},{6,70},{7,71},{8,72},{9,... | collective-permute-start | bytes 122888 | tf_op jit(solution)/shard_map/ppermute | solution.py:27
  117.1 10.2 %collective-permute-start.8 = (bf16[160,128]{1,0:T(8,128)(2,1)}, bf16[160,128]{1,0:T(8,128)(2,1)S(1)}, u32[]{:S(2)}, u32[]{:S(2)}) collective-permute-start(bf16[160,128]{1,0:T(8,128)(2,1)} %bitcast.382), channel_id=1, source_target_pairs={{0,32},{1,33},{2,34},{3,35},{4,36},{5,37},{6,38},{7,39},{8,40},{9,... | collective-permute-start | bytes 122888 | tf_op jit(solution)/shard_map/ppermute | solution.py:27
  127.4 12.5 %collective-permute-start.9 = (bf16[4,160,128]{2,1,0:T(8,128)(2,1)S(1)}, bf16[4,160,128]{2,1,0:T(8,128)(2,1)S(1)}, u32[]{:S(2)}, u32[]{:S(2)}) collective-permute-start(bf16[4,160,128]{2,1,0:T(8,128)(2,1)S(1)} %get-tuple-element.62), channel_id=1, source_target_pairs={{0,24},{1,25},{2,26},{3,27},{4,28},{5,29},{6,30},{7,31},{8,0},{9,1... | collective-permute-start | bytes 491528 | tf_op jit(solution)/shard_map/ppermute | solution.py:27
  128.2 11.6 %collective-permute-start.10 = (bf16[4,160,128]{2,1,0:T(8,128)(2,1)S(1)}, bf16[4,160,128]{2,1,0:T(8,128)(2,1)S(1)}, u32[]{:S(2)}, u32[]{:S(2)}) collective-permute-start(bf16[4,160,128]{2,1,0:T(8,128)(2,1)S(1)} %get-tuple-element.62), channel_id=1, source_target_pairs={{0,16},{1,17},{2,18},{3,19},{4,20},{5,21},{6,22},{7,23},{8,24},{9,... | collective-permute-start | bytes 491528 | tf_op jit(solution)/shard_map/ppermute | solution.py:27
  128.6 11.3 %collective-permute-start.11 = (bf16[4,160,128]{2,1,0:T(8,128)(2,1)S(1)}, bf16[4,160,128]{2,1,0:T(8,128)(2,1)S(1)}, u32[]{:S(2)}, u32[]{:S(2)}) collective-permute-start(bf16[4,160,128]{2,1,0:T(8,128)(2,1)S(1)} %get-tuple-element.62), channel_id=1, source_target_pairs={{0,8},{1,9},{2,10},{3,11},{4,12},{5,13},{6,14},{7,15},{8,16},{9,17... | collective-permute-start | bytes 491528 | tf_op jit(solution)/shard_map/ppermute | solution.py:27
  160.3 10.4 %collective-permute-start.13 = (bf16[768,4224]{1,0:T(8,128)(2,1)S(1)}, bf16[768,4224]{1,0:T(8,128)(2,1)S(1)}, u32[]{:S(2)}, u32[]{:S(2)}) collective-permute-start(bf16[768,4224]{1,0:T(8,128)(2,1)S(1)} %convolution_convert_fusion), channel_id=1, source_target_pairs={{0,1},{1,0},{2,3},{3,2},{4,5},{5,4},{6,7},{7,6},{8,9},{9,8},{10,11... | collective-permute-start | bytes 19464200 | tf_op jit(solution)/shard_map/ppermute | solution.py:27
  162.3 10.5 %collective-permute-start.23 = (bf16[128,2048]{1,0:T(8,128)(2,1)S(1)}, bf16[128,2048]{1,0:T(8,128)(2,1)S(1)}, u32[]{:S(2)}, u32[]{:S(2)}) collective-permute-start(bf16[128,2048]{1,0:T(8,128)(2,1)S(1)} %fusion.30), channel_id=1, source_target_pairs={{0,32},{1,97},{2,34},{3,99},{4,36},{5,101},{6,38},{7,103},{8,40},{... | collective-permute-start | bytes 1572872 | tf_op jit(solution)/shard_map/ppermute | solution.py:35
  164.2 14.5 %collective-permute-start.26 = (bf16[128,2176]{1,0:T(8,128)(2,1)S(1)}, bf16[128,2176]{1,0:T(8,128)(2,1)S(1)}, u32[]{:S(2)}, u32[]{:S(2)}) collective-permute-start(bf16[128,2176]{1,0:T(8,128)(2,1)S(1)} %fusion.10), channel_id=1, source_target_pairs={{0,32},{1,97},{2,34},{3,99},{4,36},{5,101},{6,38},{7,103},{8,40},{... | collective-permute-start | bytes 1671176 | tf_op jit(solution)/shard_map/ppermute | solution.py:35
  164.3 15.6 %collective-permute-start.14 = (bf16[128,2048]{1,0:T(8,128)(2,1)S(1)}, bf16[128,2048]{1,0:T(8,128)(2,1)S(1)}, u32[]{:S(2)}, u32[]{:S(2)}) collective-permute-start(bf16[128,2048]{1,0:T(8,128)(2,1)S(1)} %fusion.29), channel_id=1, source_target_pairs={{0,8},{1,25},{2,10},{3,27},{4,12},{5,29},{6,14},{7,31},{8,16},{9,1... | collective-permute-start | bytes 1572872 | tf_op jit(solution)/shard_map/ppermute | solution.py:35
  166.4 16.3 %collective-permute-start.17 = (bf16[128,2176]{1,0:T(8,128)(2,1)S(1)}, bf16[128,2176]{1,0:T(8,128)(2,1)S(1)}, u32[]{:S(2)}, u32[]{:S(2)}) collective-permute-start(bf16[128,2176]{1,0:T(8,128)(2,1)S(1)} %fusion.9), channel_id=1, source_target_pairs={{0,8},{1,25},{2,10},{3,27},{4,12},{5,29},{6,14},{7,31},{8,16},{9,1... | collective-permute-start | bytes 1671176 | tf_op jit(solution)/shard_map/ppermute | solution.py:35
  173.1 12.0 %collective-permute-start.24 = (bf16[128,2048]{1,0:T(8,128)(2,1)S(1)}, bf16[128,2048]{1,0:T(8,128)(2,1)S(1)}, u32[]{:S(2)}, u32[]{:S(2)}) collective-permute-start(bf16[128,2048]{1,0:T(8,128)(2,1)S(1)} %fusion.34), channel_id=1, source_target_pairs={{0,32},{1,97},{2,34},{3,99},{4,36},{5,101},{6,38},{7,103},{8,40},{... | collective-permute-start | bytes 1572872 | tf_op jit(solution)/shard_map/ppermute | solution.py:35
  179.2 13.0 %collective-permute-start.27 = (bf16[128,2176]{1,0:T(8,128)(2,1)S(1)}, bf16[128,2176]{1,0:T(8,128)(2,1)S(1)}, u32[]{:S(2)}, u32[]{:S(2)}) collective-permute-start(bf16[128,2176]{1,0:T(8,128)(2,1)S(1)} %fusion.5), channel_id=1, source_target_pairs={{0,32},{1,97},{2,34},{3,99},{4,36},{5,101},{6,38},{7,103},{8,40},{... | collective-permute-start | bytes 1671176 | tf_op jit(solution)/shard_map/ppermute | solution.py:35
  180.2 10.7 %collective-permute-start.15 = (bf16[128,2048]{1,0:T(8,128)(2,1)S(1)}, bf16[128,2048]{1,0:T(8,128)(2,1)S(1)}, u32[]{:S(2)}, u32[]{:S(2)}) collective-permute-start(bf16[128,2048]{1,0:T(8,128)(2,1)S(1)} %fusion.32), channel_id=1, source_target_pairs={{0,8},{1,25},{2,10},{3,27},{4,12},{5,29},{6,14},{7,31},{8,16},{9,1... | collective-permute-start | bytes 1572872 | tf_op jit(solution)/shard_map/ppermute | solution.py:35
  183.1 13.8 %collective-permute-start.18 = (bf16[128,2176]{1,0:T(8,128)(2,1)S(1)}, bf16[128,2176]{1,0:T(8,128)(2,1)S(1)}, u32[]{:S(2)}, u32[]{:S(2)}) collective-permute-start(bf16[128,2176]{1,0:T(8,128)(2,1)S(1)} %fusion.7), channel_id=1, source_target_pairs={{0,8},{1,25},{2,10},{3,27},{4,12},{5,29},{6,14},{7,31},{8,16},{9,1... | collective-permute-start | bytes 1671176 | tf_op jit(solution)/shard_map/ppermute | solution.py:35
  185.4 12.9 %collective-permute-start.25 = (bf16[128,2048]{1,0:T(8,128)(2,1)S(1)}, bf16[128,2048]{1,0:T(8,128)(2,1)S(1)}, u32[]{:S(2)}, u32[]{:S(2)}) collective-permute-start(bf16[128,2048]{1,0:T(8,128)(2,1)S(1)} %fusion.33), channel_id=1, source_target_pairs={{0,32},{1,97},{2,34},{3,99},{4,36},{5,101},{6,38},{7,103},{8,40},{... | collective-permute-start | bytes 1572872 | tf_op jit(solution)/shard_map/ppermute | solution.py:35
  191.3 11.2 %collective-permute-start.16 = (bf16[128,2048]{1,0:T(8,128)(2,1)S(1)}, bf16[128,2048]{1,0:T(8,128)(2,1)S(1)}, u32[]{:S(2)}, u32[]{:S(2)}) collective-permute-start(bf16[128,2048]{1,0:T(8,128)(2,1)S(1)} %fusion.31), channel_id=1, source_target_pairs={{0,8},{1,25},{2,10},{3,27},{4,12},{5,29},{6,14},{7,31},{8,16},{9,1... | collective-permute-start | bytes 1572872 | tf_op jit(solution)/shard_map/ppermute | solution.py:35
  192.7 11.3 %collective-permute-start.28 = (bf16[128,2176]{1,0:T(8,128)(2,1)S(1)}, bf16[128,2176]{1,0:T(8,128)(2,1)S(1)}, u32[]{:S(2)}, u32[]{:S(2)}) collective-permute-start(bf16[128,2176]{1,0:T(8,128)(2,1)S(1)} %fusion.6), channel_id=1, source_target_pairs={{0,32},{1,97},{2,34},{3,99},{4,36},{5,101},{6,38},{7,103},{8,40},{... | collective-permute-start | bytes 1671176 | tf_op jit(solution)/shard_map/ppermute | solution.py:35
  197.4 12.4 %collective-permute-start.19 = (bf16[128,2176]{1,0:T(8,128)(2,1)S(1)}, bf16[128,2176]{1,0:T(8,128)(2,1)S(1)}, u32[]{:S(2)}, u32[]{:S(2)}) collective-permute-start(bf16[128,2176]{1,0:T(8,128)(2,1)S(1)} %fusion.8), channel_id=1, source_target_pairs={{0,8},{1,25},{2,10},{3,27},{4,12},{5,29},{6,14},{7,31},{8,16},{9,1... | collective-permute-start | bytes 1671176 | tf_op jit(solution)/shard_map/ppermute | solution.py:35
  204.4 11.9 %collective-permute-start.29 = (bf16[32,4224]{1,0:T(8,128)(2,1)S(1)}, bf16[32,4224]{1,0:T(8,128)(2,1)S(1)}, u32[]{:S(2)}, u32[]{:S(2)}) collective-permute-start(bf16[32,4224]{1,0:T(8,128)(2,1)S(1)} %pad_maximum_fusion.7), channel_id=1, source_target_pairs={{0,24},{1,9},{2,26},{3,11},{4,28},{5,13},{6,30},{7,15},{8,0},{9,17... | collective-permute-start | bytes 811016 | tf_op jit(solution)/shard_map/ppermute | solution.py:35
  206.8 11.1 %collective-permute-start.30 = (bf16[32,4224]{1,0:T(8,128)(2,1)S(1)}, bf16[32,4224]{1,0:T(8,128)(2,1)S(1)}, u32[]{:S(2)}, u32[]{:S(2)}) collective-permute-start(bf16[32,4224]{1,0:T(8,128)(2,1)S(1)} %pad_maximum_fusion.8), channel_id=1, source_target_pairs={{0,16},{1,17},{2,18},{3,19},{4,20},{5,21},{6,22},{7,23},{8,24},{9,... | collective-permute-start | bytes 811016 | tf_op jit(solution)/shard_map/ppermute | solution.py:35
  208.9 11.9 %collective-permute-start.31 = (bf16[32,4224]{1,0:T(8,128)(2,1)S(1)}, bf16[32,4224]{1,0:T(8,128)(2,1)S(1)}, u32[]{:S(2)}, u32[]{:S(2)}) collective-permute-start(bf16[32,4224]{1,0:T(8,128)(2,1)S(1)} %pad_maximum_fusion.9), channel_id=1, source_target_pairs={{0,8},{1,25},{2,10},{3,27},{4,12},{5,29},{6,14},{7,31},{8,16},{9,1... | collective-permute-start | bytes 811016 | tf_op jit(solution)/shard_map/ppermute | solution.py:35
  210.2 16.2 %collective-permute-start.20 = (bf16[32,4224]{1,0:T(8,128)(2,1)S(1)}, bf16[32,4224]{1,0:T(8,128)(2,1)S(1)}, u32[]{:S(2)}, u32[]{:S(2)}) collective-permute-start(bf16[32,4224]{1,0:T(8,128)(2,1)S(1)} %pad_maximum_fusion.4), channel_id=1, source_target_pairs={{0,96},{1,33},{2,98},{3,35},{4,100},{5,37},{6,102},{7,39},{8,104},... | collective-permute-start | bytes 811016 | tf_op jit(solution)/shard_map/ppermute | solution.py:35
  214.7 11.7 %collective-permute-start.21 = (bf16[32,4224]{1,0:T(8,128)(2,1)S(1)}, bf16[32,4224]{1,0:T(8,128)(2,1)S(1)}, u32[]{:S(2)}, u32[]{:S(2)}) collective-permute-start(bf16[32,4224]{1,0:T(8,128)(2,1)S(1)} %pad_maximum_fusion.5), channel_id=1, source_target_pairs={{0,64},{1,65},{2,66},{3,67},{4,68},{5,69},{6,70},{7,71},{8,72},{9,... | collective-permute-start | bytes 811016 | tf_op jit(solution)/shard_map/ppermute | solution.py:35
  216.3 10.0 %collective-permute-start.22 = (bf16[32,4224]{1,0:T(8,128)(2,1)S(1)}, bf16[32,4224]{1,0:T(8,128)(2,1)S(1)}, u32[]{:S(2)}, u32[]{:S(2)}) collective-permute-start(bf16[32,4224]{1,0:T(8,128)(2,1)S(1)} %pad_maximum_fusion.6), channel_id=1, source_target_pairs={{0,32},{1,97},{2,34},{3,99},{4,36},{5,101},{6,38},{7,103},{8,40},{... | collective-permute-start | bytes 811016 | tf_op jit(solution)/shard_map/ppermute | solution.py:35
  228.2 9.8 %collective-permute-start.33 = (bf16[64,1152]{1,0:T(8,128)(2,1)S(1)}, bf16[64,1152]{1,0:T(8,128)(2,1)S(1)}, u32[]{:S(2)}, u32[]{:S(2)}) collective-permute-start(bf16[64,1152]{1,0:T(8,128)(2,1)S(1)} %get-tuple-element.64), channel_id=1, source_target_pairs={{0,4},{1,5},{2,6},{3,7},{4,0},{5,1},{6,2},{7,3},{8,12},{9,13},{10,... | collective-permute-start | bytes 442376 | tf_op jit(solution)/shard_map/ppermute | solution.py:27
  (16 other events, 111.2 us)
Sparse Core Ops, SparseCore 0:
  10.5 87.5 all-gather.2
